TPU v7x, 256 devices: a whole 4x4x8 slice. The times are simulated.
256 devices in a mesh: dp: 8 (over z), point: 32 (over x, y, core).
Axes of the slice: x: 4, y: 4, z: 8, core: 2. Of those that a mesh axis runs over, the one named last changes fastest.
Arguments:
- back_points: bfloat16 [8, 131072, 256], P('dp', 'point'), may hold values from -300 to 300
- fore_points: bfloat16 [8, 131072, 256], P('dp', 'point'), may hold values from -300 to 300
- cotangent: bfloat16 [8, 131072, 256], P('dp', 'point'), may hold values from -6 to 6
- w_value: bfloat16 [256, 256], replicated, may hold values from -0.375 to 0.375
- w_slice: bfloat16 [256, 512], replicated, may hold values from -1.09375 to 1.09375
- w_temp: bfloat16 [256, 8], replicated, may hold values from -0.375 to 0.375
- w_mix: float32 [256, 32], replicated, may hold values from -1 to 1
- w_out: bfloat16 [256, 256], replicated, may hold values from -0.375 to 0.375
Outputs:
- fore_result: bfloat16 [8, 131072, 256], P('dp', 'point')
- grad_points: bfloat16 [8, 131072, 256], P('dp', 'point')
- grad_value: float32 [256, 256], P('point')
- grad_slice: float32 [256, 512], P('point')
- grad_temp: float32 [256, 8], P('point')
- mixing_gradient: float32 [256, 32], P('point')
- grad_out: float32 [256, 256], P('point')
All inputs are finite; a program needn't handle non-finite values.
Results may differ from a plain program's by a relative error of at most 0.007.
Values sent between devices are 32-bit elements; how exact they have to be, the bound alone decides.
No kernel may reach another device: no remote copies, remote signals or barrier semaphores. Data moves between devices by JAX's collectives and lax.ppermute only.
A program may use at most 128 MiB of HBM per device.

v0:
```python
import jax
import jax.numpy as jnp
from jax import lax
from jax.sharding import PartitionSpec as P

MODEL_WIDTH = 256
ATTENTION_HEADS = 8
HEAD_SIZE = 32
M = 64


epsilon = 1e-05


def project(points, w_value, w_slice, w_temp):
    local_row_count = points.shape[0]
    values = jnp.dot(points, w_value, preferred_element_type=jnp.float32).astype(jnp.bfloat16)
    logits = jnp.dot(points, w_slice, preferred_element_type=jnp.float32).reshape(
        local_row_count, ATTENTION_HEADS, M
    )
    temp_coef = jnp.dot(points, w_temp, preferred_element_type=jnp.float32)
    temper = 0.5 + jax.nn.softplus(temp_coef)
    weights = jax.nn.softmax(logits / temper[:, :, None], axis=-1)
    return (
        values.reshape(local_row_count, ATTENTION_HEADS, HEAD_SIZE),
        logits,
        temp_coef,
        temper,
        weights,
        weights.astype(jnp.bfloat16),
    )


def local_sums(per_head_layout, weights, narrow_weight_part):
    slice_numerator_sum = jnp.einsum(
        "qij,qic->ijc", narrow_weight_part, per_head_layout, preferred_element_type=jnp.float32
    )
    return (slice_numerator_sum, jnp.sum(weights, axis=0))


def slice_tokens(slice_numerator_sum, denominator, block_list):
    token_rows = slice_numerator_sum / (denominator[:, :, None] + epsilon)
    mixed_state = jnp.einsum(
        "vuf,vfl->vul", token_rows, block_list, precision=lax.Precision.HIGHEST
    ).astype(jnp.bfloat16)
    return (token_rows, mixed_state)


def deslice(narrow_weight_part, mixed_state):
    local_row_count = narrow_weight_part.shape[0]
    heads_out = jnp.einsum(
        "waf,aft->wat", narrow_weight_part, mixed_state, preferred_element_type=jnp.float32
    )
    return heads_out.astype(jnp.bfloat16).reshape(local_row_count, MODEL_WIDTH)


def contract_rows(left, right):
    return lax.dot_general(
        left, right, (((0,), (0,)), ((), ())), preferred_element_type=jnp.float32
    )


def local(back_points, fore_points, cotangent, w_value, w_slice, w_temp, w_mix, w_out):
    block_list = w_mix.reshape(ATTENTION_HEADS, HEAD_SIZE, HEAD_SIZE)
    fore_x = fore_points[0]
    back_x = back_points[0]
    cot = cotangent[0]
    local_row_count = back_x.shape[0]
    fore_heads, fore_logits, fore_coef, fore_temper, fore_weights, fore_narrow = project(
        fore_x, w_value, w_slice, w_temp
    )
    fore_numer, fore_denom = local_sums(fore_heads, fore_weights, fore_narrow)
    backward_head_split, logits, temp_coef, temper, weights, backward_narrow_part = project(
        back_x, w_value, w_slice, w_temp
    )
    back_numer, back_denom = local_sums(backward_head_split, weights, backward_narrow_part)
    output_gradient = (
        jnp.dot(cot, w_out.T, preferred_element_type=jnp.float32)
        .astype(jnp.bfloat16)
        .reshape(local_row_count, ATTENTION_HEADS, HEAD_SIZE)
    )
    local_mixed_state = jnp.einsum(
        "qij,qic->ijc", backward_narrow_part, output_gradient, preferred_element_type=jnp.float32
    )
    fore_numer, fore_denom = lax.psum((fore_numer, fore_denom), "point")
    back_numer, back_denom = lax.psum((back_numer, back_denom), "point")
    mixed_state_gradient = lax.psum(local_mixed_state, "point")
    fore_tokens, fore_mixed = slice_tokens(fore_numer, fore_denom, block_list)
    fore_desliced = deslice(fore_narrow, fore_mixed)
    fore_result = jnp.dot(fore_desliced, w_out, preferred_element_type=jnp.float32).astype(
        jnp.bfloat16
    )
    token_rows, mixed_state = slice_tokens(back_numer, back_denom, block_list)
    deslice_output = deslice(backward_narrow_part, mixed_state)
    mix_term = jnp.einsum(
        "pyk,pyz->pkz", token_rows, local_mixed_state, precision=lax.Precision.HIGHEST
    ).reshape(ATTENTION_HEADS * HEAD_SIZE, HEAD_SIZE)
    token_gradient = jnp.einsum(
        "zbu,zgu->zbg", mixed_state_gradient, block_list, precision=lax.Precision.HIGHEST
    )
    inverse_denom = 1.0 / (back_denom + epsilon)
    numerator_gradient = (token_gradient * inverse_denom[:, :, None]).astype(jnp.bfloat16)
    grad_denominator = -jnp.sum(token_gradient * token_rows, axis=-1) * inverse_denom
    weight_gradient = (
        jnp.einsum("ftu,tru->ftr", output_gradient, mixed_state, preferred_element_type=jnp.float32)
        + jnp.einsum(
            "ftu,tru->ftr",
            backward_head_split,
            numerator_gradient,
            preferred_element_type=jnp.float32,
        )
        + grad_denominator[None, :, :]
    )
    grad_score = weights * (
        weight_gradient - jnp.sum(weights * weight_gradient, axis=-1, keepdims=True)
    )
    grad_logits = (
        (grad_score / temper[:, :, None])
        .reshape(local_row_count, ATTENTION_HEADS * M)
        .astype(jnp.bfloat16)
    )
    grad_coef = (
        -jax.nn.sigmoid(temp_coef) * jnp.sum(grad_score * logits, axis=-1) / (temper * temper)
    ).astype(jnp.bfloat16)
    value_gradient = jnp.einsum(
        "waf,aft->wat", backward_narrow_part, numerator_gradient, preferred_element_type=jnp.float32
    )
    value_gradient = value_gradient.astype(jnp.bfloat16).reshape(local_row_count, MODEL_WIDTH)
    total = (
        jnp.dot(value_gradient, w_value.T, preferred_element_type=jnp.float32)
        + jnp.dot(grad_logits, w_slice.T, preferred_element_type=jnp.float32)
        + jnp.dot(grad_coef, w_temp.T, preferred_element_type=jnp.float32)
    )
    grad_points = total.astype(jnp.bfloat16)
    value_term = contract_rows(back_x, value_gradient)
    slice_term = contract_rows(back_x, grad_logits)
    temp_term = contract_rows(back_x, grad_coef)
    out_term = contract_rows(deslice_output, cot)
    summed = lax.psum((value_term, slice_term, temp_term, mix_term, out_term), "dp")
    value_rows, slice_rows, temp_rows, mix_rows, out_rows = (
        lax.psum_scatter(summed[0], "point", scatter_dimension=0, tiled=True),
        lax.psum_scatter(summed[1], "point", scatter_dimension=0, tiled=True),
        lax.psum_scatter(summed[2], "point", scatter_dimension=0, tiled=True),
        lax.psum_scatter(summed[3], "point", scatter_dimension=0, tiled=True),
        lax.psum_scatter(summed[4], "point", scatter_dimension=0, tiled=True),
    )
    return (
        fore_result[None],
        grad_points[None],
        value_rows,
        slice_rows,
        temp_rows,
        mix_rows,
        out_rows,
    )


def solution(mesh):
    in_specs = (
        P("dp", "point", None),
        P("dp", "point", None),
        P("dp", "point", None),
        P(),
        P(),
        P(),
        P(),
        P(),
    )
    out_specs = (
        P("dp", "point", None),
        P("dp", "point", None),
        P("point", None),
        P("point", None),
        P("point", None),
        P("point", None),
        P("point", None),
    )
    return jax.shard_map(local, mesh=mesh, in_specs=in_specs, out_specs=out_specs, check_vma=False)
```

profile of v0, /device:TPU:32, one launch (start us, length us, event | category | flops | bytes accessed | tf_op | source)
XLA Modules:
  0.0 560.6 jit_solution(7574703235589759764)
XLA Ops:
  7.2 2.4 fusion.42
  11.1 2.1 convolution_convert_fusion.6
  13.2 2.1 convolution_convert_fusion.1
  15.4 7.4 %fusion.55 = (f32[4096,8]{0,1:T(8,128)S(1)}, f32[4096,8,64]{0,2,1:T(8,128)}) fusion(bf16[8,64,256]{2,1,0:T(8,128)(2,1)S(1)} %bitcast.136, f32[4096,8]{0,1:T(8,128)S(1)} %fusion.42, bf16[1,4096,256]{2,1,0:T(8,128)(2,1)} %param.9), kind=kOutput, calls=%fused_computation.77 | convolution fusion | flops 1080033280 | bytes 11010048 | tf_op jit(solution)/shard_map/sub | solution.py:23
  22.8 5.0 fusion.56
  27.8 2.3 convolution_convert_fusion.3
  30.2 5.5 fusion.53
  46.3 4.5 fusion.14
  50.8 67.5 %psum.73 = f32[8,64]{1,0:T(8,128)S(1)} all-reduce(f32[8,64]{1,0:T(8,128)S(1)} %get-tuple-element.39), channel_id=1, replica_groups=mesh['dp'=8,'point'=32] {'point'}, use_global_device_ids=true, to_apply=%region_9.10 | all-reduce | flops 512 | bytes 4096 | tf_op jit(solution)/shard_map/psum | solution.py:86
  119.7 42.6 %all-reduce.7.cloned.1.call-done = (f32[8,64,32]{1,2,0:T(8,128)}, f32[8,64,32]{1,2,0:T(8,128)}, f32[8,64,32]{1,2,0:T(8,128)}) async-done(((f32[8,64,32]{1,2,0:T(8,128)}, f32[8,64,32]{1,2,0:T(8,128)}, f32[8,64,32]{1,2,0:T(8,128)}), (f32[8,64,32]{1,2,0:T(8,128)}, f32[8,64,32]{1,2,0:T(8,128)}, f32[8,64,32]{1,2,0:T(8,128)})) %all-reduce.7.cloned.1.call-update) | async-done | bytes 196624 | tf_op jit(solution)/shard_map/psum | solution.py:85
  165.5 4.2 convolution_convert_fusion
  169.8 4.5 fusion.65
  178.5 8.6 %add_add_fusion = f32[8,64,4096]{2,1,0:T(8,128)} fusion(f32[8,64,4096]{2,1,0:T(8,128)} %fusion.65, bf16[4096,8,32]{0,2,1:T(8,128)(2,1)} %bitcast.127, f32[8,64]{1,0:T(8,128)S(1)} %get-tuple-element.46, f32[8,64,32]{1,2,0:T(8,128)S(1)} %get-tuple-element.54, f32[8,64]{1,0:T(8,128)S(1)} %get-tuple-element.45), kind=kOutput, calls=%fused_computation.8 | convolution fusion | flops 138444800 | bytes 18944000 | tf_op jit(solution)/shard_map/ftu,tru->ftr/dot_general | solution.py:106
  187.0 16.9 %divide_convert_fusion = (bf16[4096,8,64]{0,2,1:T(8,128)(2,1)}, f32[4096,8]{0,1:T(8,128)S(1)}) fusion(f32[4096,8]{0,1:T(8,128)S(1)} %get-tuple-element.49, f32[4096,8,64]{0,2,1:T(8,128)} %fusion.14, f32[8,64,4096]{2,1,0:T(8,128)} %add_add_fusion, f32[4096,8,64]{0,2,1:T(8,128)} %get-tuple-element.52, f32[4096,8]{0,1:T(8,128)S(1)} %get-tuple-element.51), kind=kOutput, calls=%fused_computation.7 | output fusion | flops 18874432 | bytes 29753344 | tf_op jit(solution)/shard_map/sub | solution.py:115
  203.9 3.5 fusion.29
  207.8 129.2 %all-reduce.2 = (f32[8,64]{1,0:T(8,128)S(1)}, f32[256,8]{0,1:T(8,128)}, f32[256,32]{1,0:T(8,128)}) all-reduce(f32[8,64]{1,0:T(8,128)S(1)} %get-tuple-element.41, f32[256,8]{0,1:T(8,128)S(1)} %fusion.35, f32[256,32]{1,0:T(8,128)S(1)} %bitcast.139), channel_id=1, replica_groups=mesh['dp'=8,'point'=32] {'point'}, use_global_device_ids=true, to_apply=%region_4.5 | all-reduce | flops 10752 | bytes 86016 | tf_op jit(solution)/shard_map/psum | solution.py:85
  338.4 4.2 convolution_convert_fusion.5
  345.0 4.3 fusion.63
  349.7 3.8 fusion.5
  353.5 5.6 convolution_add_fusion.1
  359.9 4.3 fusion.6
  365.0 65.5 %reduce-scatter.13.cloned.1.call-done = f32[8,512]{1,0:T(8,128)} async-done(((f32[256,512]{1,0:T(8,128)}), f32[8,512]{1,0:T(8,128)}) %reduce-scatter.13.cloned.1.call-update) | async-done | bytes 16400
  431.4 86.6 %reduce-scatter.9.cloned.1.call-done = f32[8,256]{1,0:T(8,128)} async-done(((f32[256,256]{1,0:T(8,128)}), f32[8,256]{1,0:T(8,128)}) %reduce-scatter.9.cloned.1.call-update) | async-done | bytes 8208 | tf_op jit(solution)/shard_map/reduce_scatter | solution.py:145
  518.0 34.0 %all-reduce.4 = (f32[8,256]{0,1:T(8,128)S(1)}, f32[8,512]{0,1:T(8,128)S(1)}, f32[8,8]{0,1:T(8,128)S(1)}, f32[8,32]{1,0:T(8,128)}, f32[8,256]{1,0:T(8,128)}) all-reduce(f32[8,256]{0,1:T(8,128)S(1)} %copy.36, f32[8,512]{0,1:T(8,128)S(1)} %copy.38, ...), channel_id=1, replica_groups=mesh['dp'=8,'point'=32] {'dp'}, use_global_device_ids=true, to_apply=%region_14.15 | all-reduce | flops 8512 | bytes 68096 | tf_op jit(solution)/shard_map/psum | solution.py:139
  (96 shorter events, 29.0 us)
Async XLA Ops:
  7.2 155.1 %all-reduce.7.cloned.1.call-start = ((), (), s32[]{:S(2)}) async-start(), calls=%async_computation.6 | async-start | bytes 786432 | tf_op jit(solution)/shard_map/psum | solution.py:85
  11.1 4.2 copy-start.14
  22.8 5.0 copy-start.16
  30.2 5.6 copy-start.5
  30.2 10.7 %slice-start = ((s8[8388608]{0:T(1024)(128)(4,1)}), s8[4194304]{0:T(1024)(128)(4,1)S(1)}, s32[]{:S(2)}) async-start(s8[8388608]{0:T(1024)(128)(4,1)} %bitcast.133), calls=%async_computation.7 | async-start | bytes 8388608
  35.7 5.1 copy-start.1
  35.8 5.1 slice-start.1
  46.2 72.1 %copy-start.22 = (f32[256,32]{0,1:T(8,128)S(1)}, f32[256,32]{0,1:T(8,128)}, u32[]{:S(2)}) copy-start(f32[256,32]{0,1:T(8,128)} %param.14) | copy-start | bytes 98308
  46.2 72.2 %copy-start.26 = (u32[256]{0:T(256)S(1)}, u32[256]{0:T(256)}, u32[]{:S(2)}) copy-start(u32[256]{0:T(256)} %constant.21) | copy-start | bytes 3076
  46.3 116.1 %copy-start.15 = (f32[8,64,32]{1,2,0:T(8,128)S(1)}, f32[8,64,32]{1,2,0:T(8,128)}, u32[]{:S(2)}) copy-start(f32[8,64,32]{1,2,0:T(8,128)} %fusion.62) | copy-start | bytes 196612
  46.3 318.0 %reduce-scatter.11.cloned.1.call-start = ((), (), s32[]{:S(2)}) async-start(), calls=%async_computation.4 | async-start | bytes 270336
  118.5 55.8 %copy-start.18 = (f32[8,32,32]{1,0,2:T(8,128)}, f32[8,32,32]{1,0,2:T(8,128)S(1)}, u32[]{:S(2)}) copy-start(f32[8,32,32]{1,0,2:T(8,128)S(1)} %reshape.59) | copy-start | bytes 98308
  162.3 7.4 %copy-start.6 = (bf16[4096,256]{0,1:T(8,128)(2,1)S(1)}, bf16[4096,256]{0,1:T(8,128)(2,1)}, u32[]{:S(2)}) copy-start(bf16[4096,256]{0,1:T(8,128)(2,1)} %copy-done.5) | copy-start | bytes 6291460
  169.8 4.5 copy-start.24
  169.8 4.5 copy-start.25
  169.8 5.0 copy-start.2
  178.4 252.1 %reduce-scatter.13.cloned.1.call-start = ((), (), s32[]{:S(2)}) async-start(), calls=%async_computation.5 | async-start | bytes 540672
  203.9 133.1 %copy-start.19 = (f32[8,32,32]{1,0,2:T(8,128)S(1)}, f32[8,32,32]{1,0,2:T(8,128)}, u32[]{:S(2)}) copy-start(f32[8,32,32]{1,0,2:T(8,128)} %copy-done.18) | copy-start | bytes 98308
  337.1 5.6 copy-start.9
  337.1 5.6 copy-start.10
  345.0 4.7 copy-start.17
  349.4 168.6 %reduce-scatter.9.cloned.1.call-start = ((), (), s32[]{:S(2)}) async-start(), calls=%async_computation.3 | async-start | bytes 270336 | tf_op jit(solution)/shard_map/reduce_scatter | solution.py:145
  353.5 5.6 copy-start.23
  353.5 6.3 %copy-start.21 = (bf16[256,8]{0,1:T(8,128)(2,1)S(1)}, bf16[256,8]{0,1:T(8,128)(2,1)}, u32[]{:S(2)}) copy-start(bf16[256,8]{0,1:T(8,128)(2,1)} %param.13) | copy-start | bytes 12292
  (9 other events, 27.9 us)
Sparse Core Ops, SparseCore 0:
  46.3 115.9 all-reduce.6
  178.6 84.0 reduce-scatter.10
  349.5 80.9 reduce-scatter.12
  434.1 83.8 reduce-scatter.8
where the time goes:
time: 562 us; the launch traced here: 561 us
  blocking collectives  231 us (41%)
  waiting for transfers between devices  195 us (35%)
  matrix products  84.2 us (15%)
  other arithmetic  23.9 us (4%)
  between operations  14.8 us (3%)
  local copies, waits for them, and re-layouts  11.8 us (2%)
    psum x1, blocking collectives, local(): fore_numer, fore_denom = lax.psum((fore_numer, fore_denom), 'point')  129 us
    reduce_scatter x1, waiting for transfers between devices, local(): lax.psum_scatter(summed[4], 'point', scatter_dimension=0, tiled=True)  86.6 us
    psum x1, blocking collectives, local(): back_numer, back_denom = lax.psum((back_numer, back_denom), 'point')  67.5 us
    unnamed x6, waiting for transfers between devices  65.5 us
    psum x1, waiting for transfers between devices, local(): fore_numer, fore_denom = lax.psum((fore_numer, fore_denom), 'point')  42.6 us
    psum x1, blocking collectives, local(): lax.psum((value_term, slice_term, temp_term, mix_term, out_term), 'dp')  34 us
    sub x1, other arithmetic, local(): weight_gradient - jnp.sum(weights * weight_gradient, axis=-1, keepdims=True)  16.9 us
    sub x2, matrix products, project(): weights = jax.nn.softmax(logits / temper[:, :, None], axis=-1)  12.4 us
  transfers between devices with their start and end apart: 4, of which 3 were waited for; matrix products, arithmetic and copies ran while one was open for 11% of the time, Pallas kernels for 0%

commit v1 on v0

v1 whole, which is shorter than its diff:
```python
import functools

import jax
import jax.numpy as jnp
from jax import lax
from jax.experimental import pallas as pl
from jax.experimental.pallas import tpu as pltpu
from jax.sharding import PartitionSpec as P

MODEL_WIDTH = 256
ATTENTION_HEADS = 8
HEAD_SIZE = 32
M = 64
TILE = 2048
FIRST_TILE = 1024
GRAD_TILE = 1024
SUB = 512
LOG2_E = 1.4426950408889634
VMEM_LIMIT = 24 * 1024 * 1024


epsilon = 1e-05

CORE_SWAP = [(i, i ^ 1) for i in range(32)]


def along_x(flip):
    return [(i, i ^ (8 * flip)) for i in range(32)]


def along_y(flip):
    return [(i, i ^ (2 * flip)) for i in range(32)]


def core_halves(block, first, second):
    core = lax.axis_index("point") % 2
    own = jnp.where(core == 0, first, second)
    other = jnp.where(core == 0, second, first)
    return own + lax.ppermute(other, "point", CORE_SWAP)


def row_halves(flat):
    rows = flat.shape[0] // 2
    return core_halves(flat, flat[:rows], flat[rows:])


def pair_sum(half, pairs):
    return half + lax.ppermute(half, "point", pairs)


def quad_sum(half, pairs):
    parts = [lax.ppermute(half, "point", pairs(flip)) for flip in (1, 3, 2)]
    return half + parts[0] + parts[1] + parts[2]


def both_halves(half):
    other = lax.ppermute(half, "point", CORE_SWAP)
    core = lax.axis_index("point") % 2
    return jnp.concatenate(
        [jnp.where(core == 0, half, other), jnp.where(core == 0, other, half)]
    )


def tie(*arrays):
    return lax.optimization_barrier(arrays)


def dot_nt(left, right):
    return lax.dot_general(
        left, right, (((1,), (1,)), ((), ())), preferred_element_type=jnp.float32
    )


def dot_nn(left, right):
    return jnp.dot(left, right, preferred_element_type=jnp.float32)


def dot_exact(left, right, dims):
    return lax.dot_general(
        left,
        right,
        ((dims, ((), ()))),
        precision=lax.Precision.HIGHEST,
        preferred_element_type=jnp.float32,
    )


def transpose_weights(wt, w_slice, w_value, w_temp):
    wt[0:512, :] = w_slice[...].T
    wt[512:768, :] = w_value[...].T
    wt[768:784, :] = padded_temp(w_temp).astype(jnp.bfloat16)


def padded_temp(w_temp):
    return jnp.concatenate(
        [w_temp[...].astype(jnp.float32), jnp.zeros((8, MODEL_WIDTH), jnp.float32)], axis=0
    )


def head_rows(h, size):
    return slice(h * size, (h + 1) * size)


def temper_of(coef):
    return 0.5 + jnp.maximum(coef, 0.0) + jnp.log1p(jnp.exp(-jnp.abs(coef)))


def lane_sum(w):
    total = w[:, 0:128]
    for k in range(1, w.shape[1] // 128):
        total = total + w[:, k * 128 : (k + 1) * 128]
    return total


def head_weights(logits, scale, wb, den, stats, h, columns, where=None):
    top = jnp.max(logits, axis=0, keepdims=True)
    e = jnp.exp2((logits - top) * scale)
    inv = 1.0 / jnp.sum(e, axis=0, keepdims=True)
    w = e * inv
    wb[head_rows(h, M), columns] = w.astype(jnp.bfloat16)
    den[head_rows(h, M), :] += lane_sum(w)
    if stats is not None:
        stats[h : h + 1, where] = top
        stats[8 + h : 9 + h, where] = inv


def pack_denominators(den):
    columns = [
        jnp.sum(den[head_rows(h, M), :], axis=1, keepdims=True) for h in range(ATTENTION_HEADS)
    ]
    lane = lax.broadcasted_iota(jnp.int32, (M, 128), 1)
    wide = jnp.zeros((M, 128), jnp.float32)
    for h in range(ATTENTION_HEADS):
        wide = jnp.where(lane == h, columns[h], wide)
    return jnp.concatenate(
        [wide.T[:8, :], jnp.zeros((8, M), jnp.float32)], axis=0
    )


def inverse_denominators(rows):
    tall = jnp.concatenate(
        [
            jnp.concatenate([rows, jnp.zeros((8, 128 - M), jnp.float32)], axis=1),
            jnp.zeros((120, 128), jnp.float32),
        ],
        axis=0,
    ).T
    inverse = 1.0 / (tall[:M, :] + epsilon)
    return [inverse[:, h : h + 1] for h in range(ATTENTION_HEADS)]


def back_sums_kernel(
    x_ref, cot_ref, ws_ref, wv_ref, wt_ref, wo_ref,
    sums_ref, vo_ref, stats_ref, weights_ref,
    wb, den, acc,
):
    step = pl.program_id(0)

    @pl.when(step == 0)
    def _():
        transpose_weights(weights_ref, ws_ref, wv_ref, wt_ref)
        den[...] = jnp.zeros_like(den)
        acc[...] = jnp.zeros_like(acc)

    for part in range(FIRST_TILE // SUB):
        columns = slice(part * SUB, (part + 1) * SUB)
        where = pl.ds(pl.multiple_of(step * FIRST_TILE + part * SUB, SUB), SUB)
        x = x_ref[columns, :]
        projected = dot_nt(weights_ref[...], x)
        values = projected[512:768, :].astype(jnp.bfloat16)
        out_grad = dot_nt(wo_ref[...], cot_ref[columns, :]).astype(jnp.bfloat16)
        coef = projected[768:776, :]
        inv_temper = 1.0 / temper_of(coef)
        stats_ref[16:24, where] = inv_temper
        stats_ref[24:32, where] = coef
        scale = inv_temper * LOG2_E
        for g in range(2):
            mixed_rows = []
            for j in range(4):
                h = g * 4 + j
                mixed_rows += [
                    values[head_rows(h, HEAD_SIZE), :], out_grad[head_rows(h, HEAD_SIZE), :]
                ]
                head_weights(
                    projected[head_rows(h, M), :], scale[h : h + 1, :], wb, den, stats_ref, h, columns, where
                )
            vo_ref[g * 256 : (g + 1) * 256, where] = jnp.concatenate(mixed_rows, axis=0)
    tile = pl.ds(pl.multiple_of(step * FIRST_TILE, FIRST_TILE), FIRST_TILE)
    for g in range(2):
        rows = slice(g * 256, (g + 1) * 256)
        acc[g, :, :] += dot_nt(wb[rows, :], vo_ref[rows, tile])

    @pl.when(step == pl.num_programs(0) - 1)
    def _():
        lane = lax.broadcasted_iota(jnp.int32, (M, 128), 1)
        for q in range(4):
            g, p = q // 2, q % 2
            columns = slice(128 * p, 128 * p + 128)
            even = acc[g, 128 * p : 128 * p + 64, columns]
            odd = acc[g, 128 * p + 64 : 128 * p + 128, columns]
            sums_ref[q * M : (q + 1) * M, :] = jnp.where(lane < 64, even, odd)
        sums_ref[256:272, :] = jnp.zeros((16, 128), jnp.float32)
        sums_ref[256:272, 0:M] = pack_denominators(den)


def fore_sums_kernel(x_ref, weights_ref, before_ref, *refs):
    sums_ref, wb, den, acc, values = refs[-5:]
    step = pl.program_id(0)

    @pl.when(step == 0)
    def _():
        den[...] = jnp.zeros_like(den)
        acc[...] = jnp.zeros_like(acc)

    for part in range(TILE // SUB):
        columns = slice(part * SUB, (part + 1) * SUB)
        projected = dot_nt(weights_ref[...], x_ref[columns, :])
        values[:, columns] = projected[512:768, :].astype(jnp.bfloat16)
        scale = LOG2_E / temper_of(projected[768:776, :])
        for h in range(ATTENTION_HEADS):
            head_weights(
                projected[head_rows(h, M), :], scale[h : h + 1, :], wb, den, None, h, columns
            )
    for g in range(2):
        acc[g, :, :] += dot_nt(
            wb[g * 256 : (g + 1) * 256, :], values[g * 128 : (g + 1) * 128, :]
        )

    @pl.when(step == pl.num_programs(0) - 1)
    def _():
        lane = lax.broadcasted_iota(jnp.int32, (M, 128), 1)
        for g in range(2):
            block = acc[g, 0:M, :]
            for j in range(1, 4):
                block = jnp.where(lane // HEAD_SIZE == j, acc[g, head_rows(j, M), :], block)
            rows = slice(g * M, (g + 1) * M)
            sums_ref[rows, :] = block + before_ref[rows, :]
        sums_ref[128:144, :] = jnp.zeros((16, 128), jnp.float32)
        sums_ref[128:144, 0:M] = pack_denominators(den) + before_ref[128:144, 0:M]


def back_grads_kernel(
    sums_ref, mix_ref, x_ref, cot_ref, weights_ref, vo_ref, stats_ref,
    wide_ref, gram_ref, stack_ref,
    blocks, blocks_t, shift, wb, des, dots, grads, grad_out,
):
    step = pl.program_id(0)

    @pl.when(step == 0)
    def _():
        grads[...] = jnp.zeros_like(grads)
        grad_out[...] = jnp.zeros_like(grad_out)
        blocks[...] = jnp.zeros_like(blocks)
        lane = lax.broadcasted_iota(jnp.int32, (M, 128), 1)
        first = lane % 64 < HEAD_SIZE
        inverse = inverse_denominators(sums_ref[256:264, 0:M])
        for q in range(4):
            g, p = q // 2, q % 2
            scale = jnp.where(lane < 64, inverse[2 * q], inverse[2 * q + 1])
            scaled = sums_ref[q * M : (q + 1) * M, :] * jnp.where(first, scale, 1.0)
            gram_ref[q * 128 : (q + 1) * 128, :] = dot_exact(scaled, scaled, ((0,), (0,)))
            mapped = dot_exact(scaled, mix_ref[q * 128 : (q + 1) * 128, :], ((1,), (0,)))
            product = jnp.where(first, mapped * scaled, 0.0)
            block = mapped * jnp.where(first, scale, 1.0)
            for e in range(2):
                h = 2 * q + e
                own = (lane // 64) == e
                rows = slice((h % 4) * M, (h % 4 + 1) * M)
                columns = slice(128 * p, 128 * p + 128)
                blocks[g, rows, columns] = jnp.where(own, block, 0.0).astype(jnp.bfloat16)
                gd = -jnp.sum(jnp.where(own, product, 0.0), axis=1, keepdims=True) * inverse[h]
                shift[head_rows(h, M), :] = jnp.broadcast_to(gd, (M, 128))
        for g in range(2):
            blocks_t[g, :, :] = blocks[g, :, :].T

    for part in range(GRAD_TILE // SUB):
        columns = slice(part * SUB, (part + 1) * SUB)
        where = pl.ds(pl.multiple_of(step * GRAD_TILE + part * SUB, SUB), SUB)
        logits = dot_nt(weights_ref[0:512, :], x_ref[columns, :])
        for g in range(2):
            rows = slice(g * 256, (g + 1) * 256)
            grad_w = dot_nn(blocks[g, :, :], vo_ref[rows, where])
            for j in range(4):
                h = g * 4 + j
                inv_temper = stats_ref[16 + h : 17 + h, where]
                t = logits[head_rows(h, M), :] - stats_ref[h : h + 1, where]
                w = jnp.exp2(t * (inv_temper * LOG2_E)) * stats_ref[8 + h : 9 + h, where]
                wb[head_rows(h, M), columns] = w.astype(jnp.bfloat16)
                gd = shift[head_rows(h, M), :]
                gw = grad_w[head_rows(j, M), :] + jnp.concatenate([gd] * (SUB // 128), axis=1)
                inner = jnp.sum(w * gw, axis=0, keepdims=True)
                score = w * (gw - inner)
                dots[h : h + 1, columns] = jnp.sum(score * t, axis=0, keepdims=True)
                stack_ref[head_rows(h, M), columns] = (score * inv_temper).astype(jnp.bfloat16)
    for g in range(2):
        rows = slice(g * 256, (g + 1) * 256)
        both = dot_nn(blocks_t[g, :, :], wb[rows, :]).astype(jnp.bfloat16)
        for j in range(4):
            h = g * 4 + j
            stack_ref[512 + h * 32 : 544 + h * 32, :] = both[j * 64 : j * 64 + 32, :]
            des[head_rows(h, HEAD_SIZE), :] = both[j * 64 + 32 : j * 64 + 64, :]
    tile = pl.ds(pl.multiple_of(step * GRAD_TILE, GRAD_TILE), GRAD_TILE)
    inv_temper = stats_ref[16:24, tile]
    coef = stats_ref[24:32, tile]
    grad_coef = -jax.nn.sigmoid(coef) * dots[...] * (inv_temper * inv_temper)
    stack_ref[768:784, :] = jnp.concatenate(
        [grad_coef, jnp.zeros_like(grad_coef)], axis=0
    ).astype(jnp.bfloat16)
    grads[...] += dot_nn(stack_ref[...], x_ref[...])
    grad_out[...] += dot_nn(des[...], cot_ref[...])

    @pl.when(step == pl.num_programs(0) - 1)
    def _():
        wide_ref[:, 0:256] = grads[512:768, :].T
        wide_ref[:, 256:768] = grads[0:512, :].T
        wide_ref[:, 768:1024] = grad_out[...]
        wide_ref[:, 1024:1152] = jnp.concatenate(
            [grads[768:784, :], jnp.zeros((112, MODEL_WIDTH), jnp.float32)], axis=0
        ).T


def grad_points_kernel(stack_ref, ws_ref, wv_ref, wt_ref, out_ref, wide):
    @pl.when(pl.program_id(0) == 0)
    def _():
        wide[:, 0:512] = ws_ref[...]
        wide[:, 512:768] = wv_ref[...]
        wide[:, 768:784] = padded_temp(wt_ref).T.astype(jnp.bfloat16)

    out_ref[...] = dot_nn(wide[...], stack_ref[...]).T.astype(jnp.bfloat16)


def fore_result_kernel(sums_ref, mix_ref, wb_ref, wo_ref, out_ref, blocks_t, wo_t):
    @pl.when(pl.program_id(0) == 0)
    def _():
        wo_t[...] = wo_ref[...].T
        lane = lax.broadcasted_iota(jnp.int32, (M, 128), 1)
        inverse = inverse_denominators(sums_ref[128:136, 0:M])
        for g in range(2):
            scale = jnp.zeros((M, 128), jnp.float32)
            for j in range(4):
                scale = jnp.where(lane // HEAD_SIZE == j, inverse[g * 4 + j], scale)
            tokens = sums_ref[g * M : (g + 1) * M, :] * scale
            mixed = dot_exact(tokens, mix_ref[g * 128 : (g + 1) * 128, :], ((1,), (0,)))
            rows = [jnp.where(lane // HEAD_SIZE == j, mixed, 0.0) for j in range(4)]
            blocks_t[g, :, :] = jnp.concatenate(rows, axis=0).T.astype(jnp.bfloat16)

    parts = [
        dot_nn(blocks_t[g, :, :], wb_ref[g * 256 : (g + 1) * 256, :]).astype(jnp.bfloat16)
        for g in range(2)
    ]
    out = dot_nn(wo_t[...], jnp.concatenate(parts, axis=0))
    out_ref[...] = out.T.astype(jnp.bfloat16)


def f32(*shape):
    return jax.ShapeDtypeStruct(shape, jnp.float32)


def bf16(*shape):
    return jax.ShapeDtypeStruct(shape, jnp.bfloat16)


def near(*shape, dtype=jnp.bfloat16):
    return pltpu.VMEM(shape, dtype)


def rows_of(tile, width, first=0):
    return pl.BlockSpec((tile, width), lambda i: (i + first, 0))


def columns_of(tile, rows, first=0):
    return pl.BlockSpec((rows, tile), lambda i: (0, i + first))


def whole(*shape):
    return pl.BlockSpec(shape, lambda i: (0,) * len(shape))


NEAR = pl.BlockSpec(memory_space=pltpu.VMEM)


def call(kernel, points, tile, inputs, outputs, scratch, macs, moved, aliases={}):
    operands = [
        a if spec is NEAR else pltpu.with_memory_space_constraint(a, pltpu.HBM)
        for a, spec in inputs
    ]
    return pl.pallas_call(
        kernel,
        grid=(points // tile,),
        in_specs=[spec for _, spec in inputs],
        out_specs=[spec for _, spec in outputs],
        out_shape=[shape for shape, _ in outputs],
        scratch_shapes=scratch,
        input_output_aliases=aliases,
        compiler_params=pltpu.CompilerParams(vmem_limit_bytes=VMEM_LIMIT),
        cost_estimate=pl.CostEstimate(
            flops=2 * macs * points, bytes_accessed=moved * points, transcendentals=0
        ),
    )(*operands)


def back_sums(x, cot, w_slice, w_value, w_temp, w_out):
    points = x.shape[0]
    return call(
        back_sums_kernel,
        points,
        FIRST_TILE,
        [(x, rows_of(FIRST_TILE, 256)), (cot, rows_of(FIRST_TILE, 256)),
         (w_slice, whole(256, 512)), (w_value, whole(256, 256)), (w_temp, whole(8, 256)),
         (w_out, whole(256, 256))],
        [(f32(272, 128), NEAR), (near(512, points), NEAR),
         (near(32, points, dtype=jnp.float32), NEAR), (near(784, 256), NEAR)],
        [pltpu.VMEM((512, FIRST_TILE), jnp.bfloat16), pltpu.VMEM((512, 128), jnp.float32),
         pltpu.VMEM((2, 256, 256), jnp.float32)],
        600_000,
        2200,
    )


def fore_sums(x, weights, before, wb, first, tiles):
    points = x.shape[0]
    earlier = [] if wb is None else [(wb, pl.BlockSpec(memory_space=pl.ANY))]
    return call(
        fore_sums_kernel,
        tiles * TILE,
        TILE,
        [(x, rows_of(TILE, 256, first)), (weights, NEAR), (before, NEAR)] + earlier,
        [(f32(144, 128), NEAR), (pltpu.HBM((512, points), jnp.bfloat16), columns_of(TILE, 512, first))],
        [pltpu.VMEM((512, 128), jnp.float32), pltpu.VMEM((2, 256, 128), jnp.float32),
         pltpu.VMEM((256, TILE), jnp.bfloat16)],
        500_000,
        1500,
        {} if wb is None else {3: 1},
    )


def back_grads(sums, mix, x, cot, weights, vo, stats):
    points = x.shape[0]
    tile = GRAD_TILE
    return call(
        back_grads_kernel,
        points,
        tile,
        [(sums, NEAR), (mix, NEAR), (x, rows_of(tile, 256)), (cot, rows_of(tile, 256)),
         (weights, NEAR), (vo, NEAR), (stats, NEAR)],
        [(f32(256, 1152), NEAR), (f32(512, 128), NEAR), (pltpu.HBM((784, points), jnp.bfloat16), columns_of(tile, 784))],
        [pltpu.VMEM((2, 256, 256), jnp.bfloat16), pltpu.VMEM((2, 256, 256), jnp.bfloat16),
         pltpu.VMEM((512, 128), jnp.float32), pltpu.VMEM((512, tile), jnp.bfloat16),
         pltpu.VMEM((256, tile), jnp.bfloat16), pltpu.VMEM((8, tile), jnp.float32),
         pltpu.VMEM((784, 256), jnp.float32), pltpu.VMEM((256, 256), jnp.float32)],
        800_000,
        3800,
    )


def grad_of_points(stack, w_slice, w_value, w_temp):
    points = stack.shape[1]
    return call(
        grad_points_kernel,
        points,
        TILE,
        [(stack, columns_of(TILE, 784)), (w_slice, whole(256, 512)), (w_value, whole(256, 256)),
         (w_temp, whole(8, 256))],
        [(bf16(points, 256), rows_of(TILE, 256))],
        [pltpu.VMEM((256, 784), jnp.bfloat16)],
        200_000,
        2100,
    )[0]


def fore_results(sums, mix, wb, w_out):
    points = wb.shape[1]
    return call(
        fore_result_kernel,
        points,
        TILE,
        [(sums, NEAR), (mix, NEAR), (wb, columns_of(TILE, 512)), (w_out, whole(256, 256))],
        [(bf16(points, 256), rows_of(TILE, 256))],
        [pltpu.VMEM((2, 128, 256), jnp.bfloat16), pltpu.VMEM((256, 256), jnp.bfloat16)],
        130_000,
        1600,
    )[0]


def one_hot(rows, columns, hit):
    r = lax.broadcasted_iota(jnp.int32, (rows, columns), 0)
    c = lax.broadcasted_iota(jnp.int32, (rows, columns), 1)
    return jnp.where(hit(r, c), 1.0, 0.0)


def mix_maps_kernel(turned_ref, back_ref, fore_ref):
    turned = jnp.concatenate([turned_ref[...]] * 4, axis=0)
    spread = one_hot(128, 128, lambda r, c: (r // 32 == c // 64) & (r % 32 + 32 == c % 64))
    spread_first = one_hot(128, 128, lambda r, c: (r // 32 == c // 64) & (r % 32 == c % 64))
    same = one_hot(128, 128, lambda r, c: r // 32 == c // 32)
    for g in range(2):
        blocks = jnp.where(same > 0, turned[:, g * 128 : (g + 1) * 128], 0.0)
        fore = blocks.T
        fore_ref[g * 128 : (g + 1) * 128, :] = fore
        for p in range(2):
            rows = slice(p * 64, (p + 1) * 64)
            plain = dot_exact(fore[rows, rows.start : rows.start + 64], spread[0:64, :], ((1,), (0,)))
            turn = dot_exact(
                blocks[rows, rows.start : rows.start + 64], spread_first[0:64, :], ((1,), (0,))
            )
            q = g * 2 + p
            for e in range(2):
                own = slice(e * 32, (e + 1) * 32)
                back_ref[q * 128 + e * 64 : q * 128 + e * 64 + 32, :] = plain[own, :]
                back_ref[q * 128 + e * 64 + 32 : q * 128 + e * 64 + 64, :] = turn[own, :]


def small_call(kernel, out_shape, *operands):
    return pl.pallas_call(
        kernel,
        out_shape=out_shape,
        compiler_params=pltpu.CompilerParams(vmem_limit_bytes=8 * 1024 * 1024),
    )(*operands)


def mix_maps(w_mix):
    return small_call(mix_maps_kernel, [f32(512, 128), f32(256, 128)], w_mix.T)


def own_mixing_rows(gram):
    point = lax.axis_index("point")
    odd = point // 4 % 2
    row = point // 8 * 128 + odd * 64 + point % 4 * 8
    rows = lax.dynamic_slice(gram, (row, odd * 64 + HEAD_SIZE), (8, HEAD_SIZE))
    return jnp.pad(rows, ((0, 0), (8, 88)))


def join_kernel(parts_ref, own_ref, out_ref):
    total = parts_ref[0]
    for k in range(1, 32):
        total = total + parts_ref[k]
    for k in range(8):
        out_ref[k, :, :] = total
        out_ref[k, :, 1024:1152] = total[:, 1024:1152] + own_ref[...]


def finish_kernel(parts_ref, value_ref, slice_ref, temp_ref, mix_ref, out_ref):
    total = parts_ref[0]
    for k in range(1, 8):
        total = total + parts_ref[k]
    value_ref[...] = total[:, 0:256]
    slice_ref[...] = total[:, 256:768]
    out_ref[...] = total[:, 768:1024]
    temp_ref[...] = total[:, 1024:1032]
    mix_ref[...] = total[:, 1032:1064]


def join(parts, own):
    return small_call(join_kernel, f32(8, 8, 1152), parts, own)


def finish(parts):
    shapes = [f32(8, 256), f32(8, 512), f32(8, 8), f32(8, 32), f32(8, 256)]
    return small_call(finish_kernel, shapes, parts)


def local(back_points, fore_points, cotangent, w_value, w_slice, w_temp, w_mix, w_out):
    fore_x = fore_points[0]
    back_x = back_points[0]
    cot = cotangent[0]
    turned_temp = w_temp.T

    sums, vo, stats, weights = back_sums(back_x, cot, w_slice, w_value, turned_temp, w_out)
    sums, turned_mix = tie(sums, w_mix)
    half = row_halves(sums)
    back_map, fore_map = mix_maps(turned_mix)
    half, back_map, fore = tie(half, back_map, jnp.zeros((144, 128), jnp.float32))
    half = quad_sum(half, along_x)
    fore, fore_wb = fore_sums(fore_x, weights, fore, None, 0, 1)
    half, fore = tie(half, fore)
    half = quad_sum(half, along_y)
    fore, fore_wb = fore_sums(fore_x, weights, fore, fore_wb, 1, 1)
    half, fore = tie(half, fore)
    sums = both_halves(half)
    fore_half = row_halves(fore)
    sums, fore_half = tie(sums, fore_half)
    fore_half = pair_sum(fore_half, along_x(1))

    wide, gram, stack = back_grads(sums, back_map, back_x, cot, weights, vo, stats)
    wide, gram, fore_half, turned_temp = tie(wide, gram, fore_half, turned_temp)
    parts = lax.all_to_all(wide.reshape(32, 8, 1152), "point", 0, 0)
    own_mix = own_mixing_rows(gram)
    fore_half = pair_sum(fore_half, along_x(3))
    grad_points = grad_of_points(stack, w_slice, w_value, turned_temp)
    fore_half, grad_points, own_mix = tie(fore_half, grad_points, own_mix)
    fore_half = pair_sum(fore_half, along_y(1))
    parts, fore_half = tie(parts, fore_half)
    parts = lax.all_to_all(join(parts, own_mix), "dp", 0, 0)
    fore = both_halves(pair_sum(fore_half, along_y(3)))
    fore_result = fore_results(fore, fore_map, fore_wb, w_out)
    parts, fore_result = tie(parts, fore_result)
    value_rows, slice_rows, temp_rows, mix_rows, out_rows = finish(parts)
    return (
        fore_result[None],
        grad_points[None],
        value_rows,
        slice_rows,
        temp_rows,
        mix_rows,
        out_rows,
    )


def solution(mesh):
    in_specs = (
        P("dp", "point", None),
        P("dp", "point", None),
        P("dp", "point", None),
        P(),
        P(),
        P(),
        P(),
        P(),
    )
    out_specs = (
        P("dp", "point", None),
        P("dp", "point", None),
        P("point", None),
        P("point", None),
        P("point", None),
        P("point", None),
        P("point", None),
    )
    return jax.shard_map(local, mesh=mesh, in_specs=in_specs, out_specs=out_specs, check_vma=False)
```

time: 562 us -> 95.8 us (0.17)
  blocking collectives: 231 us -> 0 us
  waiting for transfers between devices: 195 us -> 16.3 us
  matrix products: 84.2 us -> 0 us
  Pallas kernels: 0 us -> 42.6 us
  starting transfers between devices: 0.42 us -> 34.3 us
  other arithmetic: 23.9 us -> 0.16 us
  between operations: 14.8 us -> 0.82 us
  local copies, waits for them, and re-layouts: 11.8 us -> 0.16 us
    psum x3 -> x0, blocking collectives: 231 us -> none  [the longest x1 129 us: local(): fore_numer, fore_denom = lax.psum((fore_numer, fore_denom), 'point')]
    reduce_scatter x1 -> x0, waiting for transfers between devices: 86.6 us -> none  [local(): lax.psum_scatter(summed[4], 'point', scatter_dimension=0, tiled=True)]
    dot_general x26 -> x0, matrix products: 71.7 us -> none  [the longest x1 8.56 us: local(): jnp.einsum('ftu,tru->ftr', backward_head_split, numerator_gradient, prefe...]
    unnamed x6 -> x0, waiting for transfers between devices: 65.5 us -> none
    psum x1 -> x0, waiting for transfers between devices: 42.6 us -> none  [local(): fore_numer, fore_denom = lax.psum((fore_numer, fore_denom), 'point')]
    pallas_call x0 -> x9, Pallas kernels: none -> 42.6 us  [the longest x6 40.6 us: call(): pl.pallas_call(kernel, grid=(points // tile,), in_specs=[spec for _, spec...]
    ppermute x0 -> x14, starting transfers between devices: none -> 18.9 us  [the longest x4 9.6 us: pair_sum(): return half + lax.ppermute(half, 'point', pairs)]
    sub x1 -> x0, other arithmetic: 16.9 us -> none  [local(): weight_gradient - jnp.sum(weights * weight_gradient, axis=-1, keepdims=True)]
  transfers between devices with their start and end apart: 4 -> 16, of which waited for: 3 -> 7; matrix products, arithmetic and copies ran while one was open for 11% -> 0% of each run, Pallas kernels for 0% -> 36%
where the time goes in v1:
time: 95.8 us; the launch traced here: 94.3 us
  Pallas kernels  42.6 us (44%)
  starting transfers between devices  34.3 us (36%)
  waiting for transfers between devices  16.3 us (17%)
    pallas_call x6, Pallas kernels, call(): pl.pallas_call(kernel, grid=(points // tile,), in_specs=[spec for _, spec...  40.6 us
    ppermute x4, waiting for transfers between devices, pair_sum(): return half + lax.ppermute(half, 'point', pairs)  13.5 us
    ppermute x4, starting transfers between devices, pair_sum(): return half + lax.ppermute(half, 'point', pairs)  9.6 us
    ppermute x6, starting transfers between devices, quad_sum(): parts = [lax.ppermute(half, 'point', pairs(flip)) for flip in (1, 3, 2)]  8.6 us
    all_to_all x1, starting transfers between devices, local(): parts = lax.all_to_all(join(parts, own_mix), 'dp', 0, 0)  8.58 us
    all_to_all x1, starting transfers between devices, local(): parts = lax.all_to_all(wide.reshape(32, 8, 1152), 'point', 0, 0)  6.84 us
    pallas_call x3, Pallas kernels, small_call(): pl.pallas_call(kernel, out_shape=out_shape, compiler_params=pltpu.Compile...  1.94 us
  transfers between devices with their start and end apart: 16, of which 7 were waited for; matrix products, arithmetic and copies ran while one was open for 0% of the time, Pallas kernels for 36%

profile of v1, /device:TPU:32, one launch (start us, length us, event | category | flops | bytes accessed | tf_op | source)
XLA Modules:
  0.0 94.3 jit_solution(2851072241464610849)
XLA Ops:
  0.7 7.5 %shard_map.135 = (f32[272,128]{1,0:T(8,128)S(1)}, bf16[512,4096]{1,0:T(8,128)(2,1)S(1)}, f32[32,4096]{1,0:T(8,128)S(1)}, bf16[784,256]{1,0:T(8,128)(2,1)S(1)}) custom-call(bf16[4096,256]{1,0:T(8,128)(2,1)} %bitcast.15, bf16[4096,256]{1,0:T(8,128)(2,1)} %bitcast.17, bf16[256,512]{1,0:T(8,128)(2,1)} %ws_ref.3, bf16[256,256]{1,0:T(8,128)(2,1)} %wv_ref.3, ...), custom_call_target="tpu_custom_call" | custom-call | flops 4915200000 | bytes 9011200 | tf_op jit(solution)/shard_map/pallas_call | solution.py:387
  8.7 0.8 collective-permute-done
  9.5 3.1 %collective-permute-start.3 = (f32[136,128]{1,0:T(8,128)S(1)}, f32[136,128]{1,0:T(8,128)S(1)}, u32[]{:S(2)}, u32[]{:S(2)}) collective-permute-start(f32[136,128]{1,0:T(8,128)S(1)} %select_add_fusion), channel_id=1, source_target_pairs={{0,16},{1,17},{2,18},{3,19},{4,20},{5,21},{6,22},{7,23},{8,24},{9,... | collective-permute-start | bytes 208904 | tf_op jit(solution)/shard_map/ppermute | solution.py:52
  12.6 1.1 %collective-permute-start.2 = (f32[136,128]{1,0:T(8,128)S(1)}, f32[136,128]{1,0:T(8,128)S(1)}, u32[]{:S(2)}, u32[]{:S(2)}) collective-permute-start(f32[136,128]{1,0:T(8,128)S(1)} %select_add_fusion), channel_id=1, source_target_pairs={{0,24},{1,25},{2,26},{3,27},{4,28},{5,29},{6,30},{7,31},{8,16},{9,... | collective-permute-start | bytes 208904 | tf_op jit(solution)/shard_map/ppermute | solution.py:52
  13.8 4.7 %shard_map.137 = (f32[144,128]{1,0:T(8,128)S(1)}, bf16[512,4096]{1,0:T(8,128)(2,1)}) custom-call(bf16[4096,256]{1,0:T(8,128)(2,1)} %bitcast.13, bf16[784,256]{1,0:T(8,128)(2,1)S(1)} %get-tuple-element.52.weights_ref, f32[144,128]{1,0:T(8,128)S(1)} %broadcast_in_dim.9.before_ref), custom_call_target="tpu_custom_call" | custom-call | flops 2048000000 | bytes 3072000 | tf_op jit(solution)/shard_map/pallas_call | solution.py:387
  18.6 3.3 %collective-permute-start.6 = (f32[136,128]{1,0:T(8,128)S(1)}, f32[136,128]{1,0:T(8,128)S(1)}, u32[]{:S(2)}, u32[]{:S(2)}) collective-permute-start(f32[136,128]{1,0:T(8,128)S(1)} %add_add_fusion.1), channel_id=1, source_target_pairs={{0,4},{1,5},{2,6},{3,7},{4,0},{5,1},{6,2},{7,3},{8,12},{9,13},{10,... | collective-permute-start | bytes 208904 | tf_op jit(solution)/shard_map/ppermute | solution.py:52
  21.8 1.1 %collective-permute-start.5 = (f32[136,128]{1,0:T(8,128)S(1)}, f32[136,128]{1,0:T(8,128)S(1)}, u32[]{:S(2)}, u32[]{:S(2)}) collective-permute-start(f32[136,128]{1,0:T(8,128)S(1)} %add_add_fusion.1), channel_id=1, source_target_pairs={{0,6},{1,7},{2,4},{3,5},{4,2},{5,3},{6,0},{7,1},{8,14},{9,15},{10,... | collective-permute-start | bytes 208904 | tf_op jit(solution)/shard_map/ppermute | solution.py:52
  22.9 4.7 %shard_map.138 = (f32[144,128]{1,0:T(8,128)S(1)}, bf16[512,4096]{1,0:T(8,128)(2,1)}) custom-call(bf16[4096,256]{1,0:T(8,128)(2,1)} %bitcast.14, bf16[784,256]{1,0:T(8,128)(2,1)S(1)} %get-tuple-element.52.weights_ref, f32[144,128]{1,0:T(8,128)S(1)} %get-tuple-element.56.before_ref, ...), custom_call_target="tpu_custom_call", output_to_operand_aliasing={{1}: (3, {})} | custom-call | flops 2048000000 | bytes 3072000 | tf_op jit(solution)/shard_map/pallas_call | solution.py:387
  28.3 0.7 collective-permute-done.8
  29.2 2.3 %collective-permute-start.9 = (f32[72,128]{1,0:T(8,128)S(1)}, f32[72,128]{1,0:T(8,128)S(1)}, u32[]{:S(2)}, u32[]{:S(2)}) collective-permute-start(f32[72,128]{1,0:T(8,128)S(1)} %select_add_fusion.1), channel_id=1, source_target_pairs={{0,8},{1,9},{2,10},{3,11},{4,12},{5,13},{6,14},{7,15},{8,0},{9,1},... | collective-permute-start | bytes 110600 | tf_op jit(solution)/shard_map/ppermute | solution.py:48
  31.5 13.2 %shard_map.139 = (f32[256,1152]{1,0:T(8,128)}, f32[512,128]{1,0:T(8,128)S(1)}, bf16[784,4096]{1,0:T(8,128)(2,1)}) custom-call(f32[272,128]{1,0:T(8,128)S(1)} %pad_maximum_fusion.sums_ref, f32[512,128]{1,0:T(8,128)S(1)} %get-tuple-element.62.mix_ref, bf16[4096,256]{1,0:T(8,128)(2,1)} %bitcast.16, bf16[4096,256]{1,0:T(8,128)(2,1)} %bitcast.18, ...), custom_call_target="tpu_custom_call" | custom-call | flops 6553600000 | bytes 15564800 | tf_op jit(solution)/shard_map/pallas_call | solution.py:387
  44.7 6.8 %all-to-all-start = ((f32[32,8,1152]{2,1,0:T(8,128)}), f32[32,8,1152]{2,1,0:T(8,128)S(1)}, u32[]{:S(2)}, u32[]{:S(2)}) async-start(f32[32,8,1152]{2,1,0:T(8,128)} %bitcast.5), calls=%async_computation | async-start | bytes 2359296 | tf_op jit(solution)/shard_map/all_to_all | solution.py:586
  51.6 3.1 %collective-permute-start.10 = (f32[72,128]{1,0:T(8,128)S(1)}, f32[72,128]{1,0:T(8,128)S(1)}, u32[]{:S(2)}, u32[]{:S(2)}) collective-permute-start(f32[72,128]{1,0:T(8,128)S(1)} %add.79), channel_id=1, source_target_pairs={{0,24},{1,25},{2,26},{3,27},{4,28},{5,29},{6,30},{7,31},{8,16},{9,... | collective-permute-start | bytes 110600 | tf_op jit(solution)/shard_map/ppermute | solution.py:48
  54.7 5.7 %shard_map.140 = bf16[4096,256]{1,0:T(8,128)(2,1)} custom-call(bf16[784,4096]{1,0:T(8,128)(2,1)} %get-tuple-element.70.stack_ref, bf16[256,512]{1,0:T(8,128)(2,1)} %ws_ref.3, bf16[256,256]{1,0:T(8,128)(2,1)} %wv_ref.3, bf16[8,256]{1,0:T(8,128)(2,1)} %bitcast.12), custom_call_target="tpu_custom_call" | custom-call | flops 1638400000 | bytes 8601600 | tf_op jit(solution)/shard_map/pallas_call | solution.py:387
  60.6 8.5 %collective-permute-done.10 = f32[72,128]{1,0:T(8,128)S(1)} collective-permute-done((f32[72,128]{1,0:T(8,128)S(1)}, f32[72,128]{1,0:T(8,128)S(1)}, u32[]{:S(2)}, u32[]{:S(2)}) %collective-permute-start.10) | collective-permute-done | bytes 36896 | tf_op jit(solution)/shard_map/ppermute | solution.py:48
  69.1 1.5 %collective-permute-start.11 = (f32[72,128]{1,0:T(8,128)S(1)}, f32[72,128]{1,0:T(8,128)S(1)}, u32[]{:S(2)}, u32[]{:S(2)}) collective-permute-start(f32[72,128]{1,0:T(8,128)S(1)} %add.80), channel_id=1, source_target_pairs={{0,2},{1,3},{2,0},{3,1},{4,6},{5,7},{6,4},{7,5},{8,10},{9,11},{10,... | collective-permute-start | bytes 110600 | tf_op jit(solution)/shard_map/ppermute | solution.py:48
  70.6 2.5 %collective-permute-done.11 = f32[72,128]{1,0:T(8,128)S(1)} collective-permute-done((f32[72,128]{1,0:T(8,128)S(1)}, f32[72,128]{1,0:T(8,128)S(1)}, u32[]{:S(2)}, u32[]{:S(2)}) %collective-permute-start.11) | collective-permute-done | bytes 36896 | tf_op jit(solution)/shard_map/ppermute | solution.py:48
  73.1 0.8 shard_map.141
  73.9 8.6 %all-to-all-start.1 = ((f32[8,8,1152]{2,1,0:T(8,128)}), f32[8,8,1152]{2,1,0:T(8,128)S(1)}, u32[]{:S(2)}, u32[]{:S(2)}) async-start(f32[8,8,1152]{2,1,0:T(8,128)} %shard_map.141), calls=%async_computation.1 | async-start | bytes 589824 | tf_op jit(solution)/shard_map/all_to_all | solution.py:593
  82.4 2.7 %collective-permute-start.12 = (f32[72,128]{1,0:T(8,128)S(1)}, f32[72,128]{1,0:T(8,128)S(1)}, u32[]{:S(2)}, u32[]{:S(2)}) collective-permute-start(f32[72,128]{1,0:T(8,128)S(1)} %add.88), channel_id=1, source_target_pairs={{0,6},{1,7},{2,4},{3,5},{4,2},{5,3},{6,0},{7,1},{8,14},{9,15},{10,... | collective-permute-start | bytes 110600 | tf_op jit(solution)/shard_map/ppermute | solution.py:48
  85.2 2.5 %collective-permute-done.12 = f32[72,128]{1,0:T(8,128)S(1)} collective-permute-done((f32[72,128]{1,0:T(8,128)S(1)}, f32[72,128]{1,0:T(8,128)S(1)}, u32[]{:S(2)}, u32[]{:S(2)}) %collective-permute-start.12) | collective-permute-done | bytes 36896 | tf_op jit(solution)/shard_map/ppermute | solution.py:48
  87.6 1.2 %collective-permute-done.13 = f32[72,128]{1,0:T(8,128)S(1)} collective-permute-done((f32[72,128]{1,0:T(8,128)S(1)}, f32[72,128]{1,0:T(8,128)S(1)}, u32[]{:S(2)}, u32[]{:S(2)}) %collective-permute-start.13) | collective-permute-done | bytes 36896 | tf_op jit(solution)/shard_map/ppermute | solution.py:57
  88.9 4.8 %shard_map.142 = bf16[4096,256]{1,0:T(8,128)(2,1)} custom-call(f32[144,128]{1,0:T(8,128)S(1)} %pad_maximum_fusion.1.sums_ref, f32[256,128]{1,0:T(8,128)S(1)} %get-tuple-element.77.mix_ref, bf16[512,4096]{1,0:T(8,128)(2,1)} %get-tuple-element.78.wb_ref, bf16[256,256]{1,0:T(8,128)(2,1)} %wo_ref.3), custom_call_target="tpu_custom_call" | custom-call | flops 1064960000 | bytes 6553600 | tf_op jit(solution)/shard_map/pallas_call | solution.py:387
  93.7 0.7 shard_map.143
  (36 shorter events, 1.7 us)
Async XLA Ops:
  0.6 7.6 %copy-start = (f32[256,32]{0,1:T(8,128)S(1)}, f32[256,32]{0,1:T(8,128)}, u32[]{:S(2)}) copy-start(f32[256,32]{0,1:T(8,128)} %param.14) | copy-start | bytes 98308
  8.2 1.3 %collective-permute-start = (f32[136,128]{1,0:T(8,128)S(1)}, f32[136,128]{1,0:T(8,128)S(1)}, u32[]{:S(2)}, u32[]{:S(2)}) collective-permute-start(f32[136,128]{1,0:T(8,128)S(1)} %slice_select_fusion), channel_id=1, source_target_pairs={{0,1},{1,0},{2,3},{3,2},{4,5},{5,4},{6,7},{7,6},{8,9},{9,8},{10,11... | collective-permute-start | bytes 208904 | tf_op jit(solution)/shard_map/ppermute | solution.py:39
  9.5 9.0 %collective-permute-start.3 = (f32[136,128]{1,0:T(8,128)S(1)}, f32[136,128]{1,0:T(8,128)S(1)}, u32[]{:S(2)}, u32[]{:S(2)}) collective-permute-start(f32[136,128]{1,0:T(8,128)S(1)} %select_add_fusion), channel_id=1, source_target_pairs={{0,16},{1,17},{2,18},{3,19},{4,20},{5,21},{6,22},{7,23},{8,24},{9,... | collective-permute-start | bytes 208904 | tf_op jit(solution)/shard_map/ppermute | solution.py:52
  12.6 5.9 %collective-permute-start.2 = (f32[136,128]{1,0:T(8,128)S(1)}, f32[136,128]{1,0:T(8,128)S(1)}, u32[]{:S(2)}, u32[]{:S(2)}) collective-permute-start(f32[136,128]{1,0:T(8,128)S(1)} %select_add_fusion), channel_id=1, source_target_pairs={{0,24},{1,25},{2,26},{3,27},{4,28},{5,29},{6,30},{7,31},{8,16},{9,... | collective-permute-start | bytes 208904 | tf_op jit(solution)/shard_map/ppermute | solution.py:52
  13.8 4.7 %collective-permute-start.1 = (f32[136,128]{1,0:T(8,128)S(1)}, f32[136,128]{1,0:T(8,128)S(1)}, u32[]{:S(2)}, u32[]{:S(2)}) collective-permute-start(f32[136,128]{1,0:T(8,128)S(1)} %select_add_fusion), channel_id=1, source_target_pairs={{0,8},{1,9},{2,10},{3,11},{4,12},{5,13},{6,14},{7,15},{8,0},{9,1},... | collective-permute-start | bytes 208904 | tf_op jit(solution)/shard_map/ppermute | solution.py:52
  18.6 9.1 %collective-permute-start.6 = (f32[136,128]{1,0:T(8,128)S(1)}, f32[136,128]{1,0:T(8,128)S(1)}, u32[]{:S(2)}, u32[]{:S(2)}) collective-permute-start(f32[136,128]{1,0:T(8,128)S(1)} %add_add_fusion.1), channel_id=1, source_target_pairs={{0,4},{1,5},{2,6},{3,7},{4,0},{5,1},{6,2},{7,3},{8,12},{9,13},{10,... | collective-permute-start | bytes 208904 | tf_op jit(solution)/shard_map/ppermute | solution.py:52
  21.8 5.8 %collective-permute-start.5 = (f32[136,128]{1,0:T(8,128)S(1)}, f32[136,128]{1,0:T(8,128)S(1)}, u32[]{:S(2)}, u32[]{:S(2)}) collective-permute-start(f32[136,128]{1,0:T(8,128)S(1)} %add_add_fusion.1), channel_id=1, source_target_pairs={{0,6},{1,7},{2,4},{3,5},{4,2},{5,3},{6,0},{7,1},{8,14},{9,15},{10,... | collective-permute-start | bytes 208904 | tf_op jit(solution)/shard_map/ppermute | solution.py:52
  22.9 4.8 %collective-permute-start.4 = (f32[136,128]{1,0:T(8,128)S(1)}, f32[136,128]{1,0:T(8,128)S(1)}, u32[]{:S(2)}, u32[]{:S(2)}) collective-permute-start(f32[136,128]{1,0:T(8,128)S(1)} %add_add_fusion.1), channel_id=1, source_target_pairs={{0,2},{1,3},{2,0},{3,1},{4,6},{5,7},{6,4},{7,5},{8,10},{9,11},{10,... | collective-permute-start | bytes 208904 | tf_op jit(solution)/shard_map/ppermute | solution.py:52
  27.7 1.3 %collective-permute-start.8 = (f32[72,128]{1,0:T(8,128)S(1)}, f32[72,128]{1,0:T(8,128)S(1)}, u32[]{:S(2)}, u32[]{:S(2)}) collective-permute-start(f32[72,128]{1,0:T(8,128)S(1)} %slice_select_fusion.1), channel_id=1, source_target_pairs={{0,1},{1,0},{2,3},{3,2},{4,5},{5,4},{6,7},{7,6},{8,9},{9,8},{10,11... | collective-permute-start | bytes 110600 | tf_op jit(solution)/shard_map/ppermute | solution.py:39
  27.8 1.4 %collective-permute-start.7 = (f32[136,128]{1,0:T(8,128)S(1)}, f32[136,128]{1,0:T(8,128)S(1)}, u32[]{:S(2)}, u32[]{:S(2)}) collective-permute-start(f32[136,128]{1,0:T(8,128)S(1)} %add_add_fusion), channel_id=1, source_target_pairs={{0,1},{1,0},{2,3},{3,2},{4,5},{5,4},{6,7},{7,6},{8,9},{9,8},{10,11... | collective-permute-start | bytes 208904 | tf_op jit(solution)/shard_map/ppermute | solution.py:57
  29.2 15.4 %collective-permute-start.9 = (f32[72,128]{1,0:T(8,128)S(1)}, f32[72,128]{1,0:T(8,128)S(1)}, u32[]{:S(2)}, u32[]{:S(2)}) collective-permute-start(f32[72,128]{1,0:T(8,128)S(1)} %select_add_fusion.1), channel_id=1, source_target_pairs={{0,8},{1,9},{2,10},{3,11},{4,12},{5,13},{6,14},{7,15},{8,0},{9,1},... | collective-permute-start | bytes 110600 | tf_op jit(solution)/shard_map/ppermute | solution.py:48
  44.7 28.4 %all-to-all-start = ((f32[32,8,1152]{2,1,0:T(8,128)}), f32[32,8,1152]{2,1,0:T(8,128)S(1)}, u32[]{:S(2)}, u32[]{:S(2)}) async-start(f32[32,8,1152]{2,1,0:T(8,128)} %bitcast.5), calls=%async_computation | async-start | bytes 2359296 | tf_op jit(solution)/shard_map/all_to_all | solution.py:586
  51.6 17.5 %collective-permute-start.10 = (f32[72,128]{1,0:T(8,128)S(1)}, f32[72,128]{1,0:T(8,128)S(1)}, u32[]{:S(2)}, u32[]{:S(2)}) collective-permute-start(f32[72,128]{1,0:T(8,128)S(1)} %add.79), channel_id=1, source_target_pairs={{0,24},{1,25},{2,26},{3,27},{4,28},{5,29},{6,30},{7,31},{8,16},{9,... | collective-permute-start | bytes 110600 | tf_op jit(solution)/shard_map/ppermute | solution.py:48
  69.1 4.0 %collective-permute-start.11 = (f32[72,128]{1,0:T(8,128)S(1)}, f32[72,128]{1,0:T(8,128)S(1)}, u32[]{:S(2)}, u32[]{:S(2)}) collective-permute-start(f32[72,128]{1,0:T(8,128)S(1)} %add.80), channel_id=1, source_target_pairs={{0,2},{1,3},{2,0},{3,1},{4,6},{5,7},{6,4},{7,5},{8,10},{9,11},{10,... | collective-permute-start | bytes 110600 | tf_op jit(solution)/shard_map/ppermute | solution.py:48
  73.9 19.8 %all-to-all-start.1 = ((f32[8,8,1152]{2,1,0:T(8,128)}), f32[8,8,1152]{2,1,0:T(8,128)S(1)}, u32[]{:S(2)}, u32[]{:S(2)}) async-start(f32[8,8,1152]{2,1,0:T(8,128)} %shard_map.141), calls=%async_computation.1 | async-start | bytes 589824 | tf_op jit(solution)/shard_map/all_to_all | solution.py:593
  82.4 5.2 %collective-permute-start.12 = (f32[72,128]{1,0:T(8,128)S(1)}, f32[72,128]{1,0:T(8,128)S(1)}, u32[]{:S(2)}, u32[]{:S(2)}) collective-permute-start(f32[72,128]{1,0:T(8,128)S(1)} %add.88), channel_id=1, source_target_pairs={{0,6},{1,7},{2,4},{3,5},{4,2},{5,3},{6,0},{7,1},{8,14},{9,15},{10,... | collective-permute-start | bytes 110600 | tf_op jit(solution)/shard_map/ppermute | solution.py:48
  87.6 1.2 %collective-permute-start.13 = (f32[72,128]{1,0:T(8,128)S(1)}, f32[72,128]{1,0:T(8,128)S(1)}, u32[]{:S(2)}, u32[]{:S(2)}) collective-permute-start(f32[72,128]{1,0:T(8,128)S(1)} %add.89), channel_id=1, source_target_pairs={{0,1},{1,0},{2,3},{3,2},{4,5},{5,4},{6,7},{7,6},{8,9},{9,8},{10,11... | collective-permute-start | bytes 110600 | tf_op jit(solution)/shard_map/ppermute | solution.py:57

commit v2 on v1

--- a/solution.py
+++ b/solution.py
@@ -13,10 +13,11 @@
 M = 64
 TILE = 2048
 FIRST_TILE = 1024
+FIRST_SUB = 512
 GRAD_TILE = 1024
 SUB = 512
 LOG2_E = 1.4426950408889634
-VMEM_LIMIT = 24 * 1024 * 1024
+VMEM_LIMIT = 20 * 1024 * 1024
 
 
 epsilon = 1e-05
@@ -32,16 +33,11 @@
     return [(i, i ^ (2 * flip)) for i in range(32)]
 
 
-def core_halves(block, first, second):
-    core = lax.axis_index("point") % 2
-    own = jnp.where(core == 0, first, second)
-    other = jnp.where(core == 0, second, first)
+def row_halves(flat, even):
+    rows = flat.shape[0] // 2
+    own = jnp.where(even, flat[:rows], flat[rows:])
+    other = jnp.where(even, flat[rows:], flat[:rows])
     return own + lax.ppermute(other, "point", CORE_SWAP)
-
-
-def row_halves(flat):
-    rows = flat.shape[0] // 2
-    return core_halves(flat, flat[:rows], flat[rows:])
 
 
 def pair_sum(half, pairs):
@@ -53,12 +49,9 @@
     return half + parts[0] + parts[1] + parts[2]
 
 
-def both_halves(half):
+def both_halves(half, even):
     other = lax.ppermute(half, "point", CORE_SWAP)
-    core = lax.axis_index("point") % 2
-    return jnp.concatenate(
-        [jnp.where(core == 0, half, other), jnp.where(core == 0, other, half)]
-    )
+    return jnp.concatenate([jnp.where(even, half, other), jnp.where(even, other, half)])
 
 
 def tie(*arrays):
@@ -112,16 +105,16 @@
     return total
 
 
-def head_weights(logits, scale, wb, den, stats, h, columns, where=None):
-    top = jnp.max(logits, axis=0, keepdims=True)
-    e = jnp.exp2((logits - top) * scale)
+def head_weights(logits, scale, wb, den, kept, h, columns, where=None):
+    below = logits - jnp.max(logits, axis=0, keepdims=True)
+    e = jnp.exp2(below * scale)
     inv = 1.0 / jnp.sum(e, axis=0, keepdims=True)
     w = e * inv
     wb[head_rows(h, M), columns] = w.astype(jnp.bfloat16)
     den[head_rows(h, M), :] += lane_sum(w)
-    if stats is not None:
-        stats[h : h + 1, where] = top
-        stats[8 + h : 9 + h, where] = inv
+    if kept is not None:
+        kept[0][head_rows(h, M), where] = w
+        kept[1][head_rows(h, M), where] = below
 
 
 def pack_denominators(den):
@@ -150,104 +143,116 @@
 
 
 def back_sums_kernel(
-    x_ref, cot_ref, ws_ref, wv_ref, wt_ref, wo_ref,
-    sums_ref, vo_ref, stats_ref, weights_ref,
-    wb, den, acc,
+    x_far, cot_far, ws_far, wv_far, wt_far, wo_far, fore_far,
+    sums_ref, vo_ref, stats_ref, w_ref, below_ref, weights_ref, x_ref, cot_ref, fore_ref,
+    wb, den, acc, ws, wv, wt, wo, sems,
+):
+    chunks = x_ref.shape[0] // FIRST_TILE
+
+    def fetch(source, target, k):
+        copy = pltpu.make_async_copy(source, target, sems.at[k])
+        copy.start()
+        return copy
+
+    small = [fetch(a, b, k) for k, (a, b) in enumerate(
+        [(ws_far, ws), (wv_far, wv), (wt_far, wt), (wo_far, wo)]
+    )]
+    large = []
+    for c in range(chunks):
+        rows = pl.ds(c * FIRST_TILE, FIRST_TILE)
+        large.append((
+            fetch(x_far.at[rows], x_ref.at[rows], 4 + 2 * c),
+            fetch(cot_far.at[rows], cot_ref.at[rows], 5 + 2 * c),
+        ))
+    fore_copy = fetch(fore_far, fore_ref, 4 + 2 * chunks)
+    den[...] = jnp.zeros_like(den)
+    acc[...] = jnp.zeros_like(acc)
+    for copy in small:
+        copy.wait()
+    transpose_weights(weights_ref, ws, wv, wt)
+    for c in range(chunks):
+        for copy in large[c]:
+            copy.wait()
+        for part in range(FIRST_TILE // FIRST_SUB):
+            columns = slice(part * FIRST_SUB, (part + 1) * FIRST_SUB)
+            where = slice(c * FIRST_TILE + part * FIRST_SUB, c * FIRST_TILE + (part + 1) * FIRST_SUB)
+            projected = dot_nt(weights_ref[...], x_ref[where, :])
+            values = projected[512:768, :].astype(jnp.bfloat16)
+            out_grad = dot_nt(wo[...], cot_ref[where, :]).astype(jnp.bfloat16)
+            coef = projected[768:776, :]
+            inv_temper = 1.0 / temper_of(coef)
+            stats_ref[0:8, where] = inv_temper
+            stats_ref[8:16, where] = coef
+            scale = inv_temper * LOG2_E
+            for g in range(2):
+                mixed_rows = []
+                for j in range(4):
+                    h = g * 4 + j
+                    mixed_rows += [
+                        values[head_rows(h, HEAD_SIZE), :], out_grad[head_rows(h, HEAD_SIZE), :]
+                    ]
+                    head_weights(
+                        projected[head_rows(h, M), :], scale[h : h + 1, :], wb, den,
+                        (w_ref, below_ref), h, columns, where,
+                    )
+                vo_ref[g * 256 : (g + 1) * 256, where] = jnp.concatenate(mixed_rows, axis=0)
+        tile = slice(c * FIRST_TILE, (c + 1) * FIRST_TILE)
+        for g in range(2):
+            rows = slice(g * 256, (g + 1) * 256)
+            acc[g, :, :] += dot_nt(wb[rows, :], vo_ref[rows, tile])
+
+    lane = lax.broadcasted_iota(jnp.int32, (M, 128), 1)
+    for q in range(4):
+        g, p = q // 2, q % 2
+        columns = slice(128 * p, 128 * p + 128)
+        even = acc[g, 128 * p : 128 * p + 64, columns]
+        odd = acc[g, 128 * p + 64 : 128 * p + 128, columns]
+        sums_ref[q * M : (q + 1) * M, :] = jnp.where(lane < 64, even, odd)
+    sums_ref[256:272, :] = jnp.zeros((16, 128), jnp.float32)
+    sums_ref[256:272, 0:M] = pack_denominators(den)
+    fore_copy.wait()
+
+
+def fore_sums_kernel(x_ref, weights_ref, sums_ref, wb, den, acc, values):
+    den[...] = jnp.zeros_like(den)
+    acc[...] = jnp.zeros_like(acc)
+    for c in range(x_ref.shape[0] // TILE):
+        for part in range(TILE // SUB):
+            columns = slice(part * SUB, (part + 1) * SUB)
+            where = slice(c * TILE + part * SUB, c * TILE + (part + 1) * SUB)
+            projected = dot_nt(weights_ref[...], x_ref[where, :])
+            values[:, columns] = projected[512:768, :].astype(jnp.bfloat16)
+            scale = LOG2_E / temper_of(projected[768:776, :])
+            for h in range(ATTENTION_HEADS):
+                head_weights(
+                    projected[head_rows(h, M), :], scale[h : h + 1, :], wb, den, None, h, where
+                )
+        for g in range(2):
+            acc[g, :, :] += dot_nt(
+                wb[g * 256 : (g + 1) * 256, c * TILE : (c + 1) * TILE],
+                values[g * 128 : (g + 1) * 128, :],
+            )
+
+    lane = lax.broadcasted_iota(jnp.int32, (M, 128), 1)
+    for g in range(2):
+        block = acc[g, 0:M, :]
+        for j in range(1, 4):
+            block = jnp.where(lane // HEAD_SIZE == j, acc[g, head_rows(j, M), :], block)
+        sums_ref[g * M : (g + 1) * M, :] = block
+    sums_ref[128:144, :] = jnp.zeros((16, 128), jnp.float32)
+    sums_ref[128:144, 0:M] = pack_denominators(den)
+
+
+def back_grads_kernel(
+    sums_ref, mix_ref, x_ref, cot_ref, vo_ref, stats_ref, w_ref, below_ref, fore_wb,
+    keep_ref, send_ref, stack_ref, fore_far,
+    blocks, blocks_t, shift, wb, des, dots, grads, grad_out, wide, sem,
 ):
     step = pl.program_id(0)
 
     @pl.when(step == 0)
     def _():
-        transpose_weights(weights_ref, ws_ref, wv_ref, wt_ref)
-        den[...] = jnp.zeros_like(den)
-        acc[...] = jnp.zeros_like(acc)
-
-    for part in range(FIRST_TILE // SUB):
-        columns = slice(part * SUB, (part + 1) * SUB)
-        where = pl.ds(pl.multiple_of(step * FIRST_TILE + part * SUB, SUB), SUB)
-        x = x_ref[columns, :]
-        projected = dot_nt(weights_ref[...], x)
-        values = projected[512:768, :].astype(jnp.bfloat16)
-        out_grad = dot_nt(wo_ref[...], cot_ref[columns, :]).astype(jnp.bfloat16)
-        coef = projected[768:776, :]
-        inv_temper = 1.0 / temper_of(coef)
-        stats_ref[16:24, where] = inv_temper
-        stats_ref[24:32, where] = coef
-        scale = inv_temper * LOG2_E
-        for g in range(2):
-            mixed_rows = []
-            for j in range(4):
-                h = g * 4 + j
-                mixed_rows += [
-                    values[head_rows(h, HEAD_SIZE), :], out_grad[head_rows(h, HEAD_SIZE), :]
-                ]
-                head_weights(
-                    projected[head_rows(h, M), :], scale[h : h + 1, :], wb, den, stats_ref, h, columns, where
-                )
-            vo_ref[g * 256 : (g + 1) * 256, where] = jnp.concatenate(mixed_rows, axis=0)
-    tile = pl.ds(pl.multiple_of(step * FIRST_TILE, FIRST_TILE), FIRST_TILE)
-    for g in range(2):
-        rows = slice(g * 256, (g + 1) * 256)
-        acc[g, :, :] += dot_nt(wb[rows, :], vo_ref[rows, tile])
-
-    @pl.when(step == pl.num_programs(0) - 1)
-    def _():
-        lane = lax.broadcasted_iota(jnp.int32, (M, 128), 1)
-        for q in range(4):
-            g, p = q // 2, q % 2
-            columns = slice(128 * p, 128 * p + 128)
-            even = acc[g, 128 * p : 128 * p + 64, columns]
-            odd = acc[g, 128 * p + 64 : 128 * p + 128, columns]
-            sums_ref[q * M : (q + 1) * M, :] = jnp.where(lane < 64, even, odd)
-        sums_ref[256:272, :] = jnp.zeros((16, 128), jnp.float32)
-        sums_ref[256:272, 0:M] = pack_denominators(den)
-
-
-def fore_sums_kernel(x_ref, weights_ref, before_ref, *refs):
-    sums_ref, wb, den, acc, values = refs[-5:]
-    step = pl.program_id(0)
-
-    @pl.when(step == 0)
-    def _():
-        den[...] = jnp.zeros_like(den)
-        acc[...] = jnp.zeros_like(acc)
-
-    for part in range(TILE // SUB):
-        columns = slice(part * SUB, (part + 1) * SUB)
-        projected = dot_nt(weights_ref[...], x_ref[columns, :])
-        values[:, columns] = projected[512:768, :].astype(jnp.bfloat16)
-        scale = LOG2_E / temper_of(projected[768:776, :])
-        for h in range(ATTENTION_HEADS):
-            head_weights(
-                projected[head_rows(h, M), :], scale[h : h + 1, :], wb, den, None, h, columns
-            )
-    for g in range(2):
-        acc[g, :, :] += dot_nt(
-            wb[g * 256 : (g + 1) * 256, :], values[g * 128 : (g + 1) * 128, :]
-        )
-
-    @pl.when(step == pl.num_programs(0) - 1)
-    def _():
-        lane = lax.broadcasted_iota(jnp.int32, (M, 128), 1)
-        for g in range(2):
-            block = acc[g, 0:M, :]
-            for j in range(1, 4):
-                block = jnp.where(lane // HEAD_SIZE == j, acc[g, head_rows(j, M), :], block)
-            rows = slice(g * M, (g + 1) * M)
-            sums_ref[rows, :] = block + before_ref[rows, :]
-        sums_ref[128:144, :] = jnp.zeros((16, 128), jnp.float32)
-        sums_ref[128:144, 0:M] = pack_denominators(den) + before_ref[128:144, 0:M]
-
-
-def back_grads_kernel(
-    sums_ref, mix_ref, x_ref, cot_ref, weights_ref, vo_ref, stats_ref,
-    wide_ref, gram_ref, stack_ref,
-    blocks, blocks_t, shift, wb, des, dots, grads, grad_out,
-):
-    step = pl.program_id(0)
-
-    @pl.when(step == 0)
-    def _():
+        pltpu.make_async_copy(fore_wb, fore_far, sem).start()
         grads[...] = jnp.zeros_like(grads)
         grad_out[...] = jnp.zeros_like(grad_out)
         blocks[...] = jnp.zeros_like(blocks)
@@ -258,7 +263,6 @@
             g, p = q // 2, q % 2
             scale = jnp.where(lane < 64, inverse[2 * q], inverse[2 * q + 1])
             scaled = sums_ref[q * M : (q + 1) * M, :] * jnp.where(first, scale, 1.0)
-            gram_ref[q * 128 : (q + 1) * 128, :] = dot_exact(scaled, scaled, ((0,), (0,)))
             mapped = dot_exact(scaled, mix_ref[q * 128 : (q + 1) * 128, :], ((1,), (0,)))
             product = jnp.where(first, mapped * scaled, 0.0)
             block = mapped * jnp.where(first, scale, 1.0)
@@ -276,22 +280,21 @@
     for part in range(GRAD_TILE // SUB):
         columns = slice(part * SUB, (part + 1) * SUB)
         where = pl.ds(pl.multiple_of(step * GRAD_TILE + part * SUB, SUB), SUB)
-        logits = dot_nt(weights_ref[0:512, :], x_ref[columns, :])
         for g in range(2):
             rows = slice(g * 256, (g + 1) * 256)
             grad_w = dot_nn(blocks[g, :, :], vo_ref[rows, where])
             for j in range(4):
                 h = g * 4 + j
-                inv_temper = stats_ref[16 + h : 17 + h, where]
-                t = logits[head_rows(h, M), :] - stats_ref[h : h + 1, where]
-                w = jnp.exp2(t * (inv_temper * LOG2_E)) * stats_ref[8 + h : 9 + h, where]
+                w = w_ref[head_rows(h, M), where]
                 wb[head_rows(h, M), columns] = w.astype(jnp.bfloat16)
                 gd = shift[head_rows(h, M), :]
                 gw = grad_w[head_rows(j, M), :] + jnp.concatenate([gd] * (SUB // 128), axis=1)
                 inner = jnp.sum(w * gw, axis=0, keepdims=True)
-                score = w * (gw - inner)
-                dots[h : h + 1, columns] = jnp.sum(score * t, axis=0, keepdims=True)
-                stack_ref[head_rows(h, M), columns] = (score * inv_temper).astype(jnp.bfloat16)
+                grad = w * ((gw - inner) * stats_ref[h : h + 1, where])
+                dots[h : h + 1, columns] = jnp.sum(
+                    grad * below_ref[head_rows(h, M), where], axis=0, keepdims=True
+                )
+                stack_ref[head_rows(h, M), columns] = grad.astype(jnp.bfloat16)
     for g in range(2):
         rows = slice(g * 256, (g + 1) * 256)
         both = dot_nn(blocks_t[g, :, :], wb[rows, :]).astype(jnp.bfloat16)
@@ -300,23 +303,28 @@
             stack_ref[512 + h * 32 : 544 + h * 32, :] = both[j * 64 : j * 64 + 32, :]
             des[head_rows(h, HEAD_SIZE), :] = both[j * 64 + 32 : j * 64 + 64, :]
     tile = pl.ds(pl.multiple_of(step * GRAD_TILE, GRAD_TILE), GRAD_TILE)
-    inv_temper = stats_ref[16:24, tile]
-    coef = stats_ref[24:32, tile]
-    grad_coef = -jax.nn.sigmoid(coef) * dots[...] * (inv_temper * inv_temper)
+    grad_coef = -jax.nn.sigmoid(stats_ref[8:16, tile]) * dots[...] * stats_ref[0:8, tile]
     stack_ref[768:784, :] = jnp.concatenate(
         [grad_coef, jnp.zeros_like(grad_coef)], axis=0
     ).astype(jnp.bfloat16)
-    grads[...] += dot_nn(stack_ref[...], x_ref[...])
-    grad_out[...] += dot_nn(des[...], cot_ref[...])
+    grads[...] += dot_nn(stack_ref[...], x_ref[tile, :])
+    grad_out[...] += dot_nn(des[...], cot_ref[tile, :])
 
     @pl.when(step == pl.num_programs(0) - 1)
     def _():
-        wide_ref[:, 0:256] = grads[512:768, :].T
-        wide_ref[:, 256:768] = grads[0:512, :].T
-        wide_ref[:, 768:1024] = grad_out[...]
-        wide_ref[:, 1024:1152] = jnp.concatenate(
+        wide[:, 0:256] = grads[512:768, :].T
+        wide[:, 256:768] = grads[0:512, :].T
+        wide[:, 768:1024] = grad_out[...]
+        wide[:, 1024:1152] = jnp.concatenate(
             [grads[768:784, :], jnp.zeros((112, MODEL_WIDTH), jnp.float32)], axis=0
         ).T
+        core = lax.rem(lax.axis_index("point"), 2)
+        for chip in range(16):
+            own = pl.multiple_of((chip * 2 + core) * 8, 8)
+            other = pl.multiple_of((chip * 2 + 1 - core) * 8, 8)
+            keep_ref[chip, :, :] = wide[pl.ds(own, 8), :]
+            send_ref[chip, :, :] = wide[pl.ds(other, 8), :]
+        pltpu.make_async_copy(fore_wb, fore_far, sem).wait()
 
 
 def grad_points_kernel(stack_ref, ws_ref, wv_ref, wt_ref, out_ref, wide):
@@ -399,55 +407,72 @@
     )(*operands)
 
 
-def back_sums(x, cot, w_slice, w_value, w_temp, w_out):
+def back_sums(x, cot, w_slice, w_value, w_temp, w_out, fore_x):
     points = x.shape[0]
-    return call(
+    operands = [
+        pltpu.with_memory_space_constraint(a, pltpu.HBM)
+        for a in (x, cot, w_slice, w_value, w_temp, w_out, fore_x)
+    ]
+    wide = functools.partial(near, dtype=jnp.float32)
+    return pl.pallas_call(
         back_sums_kernel,
-        points,
-        FIRST_TILE,
-        [(x, rows_of(FIRST_TILE, 256)), (cot, rows_of(FIRST_TILE, 256)),
-         (w_slice, whole(256, 512)), (w_value, whole(256, 256)), (w_temp, whole(8, 256)),
-         (w_out, whole(256, 256))],
-        [(f32(272, 128), NEAR), (near(512, points), NEAR),
-         (near(32, points, dtype=jnp.float32), NEAR), (near(784, 256), NEAR)],
-        [pltpu.VMEM((512, FIRST_TILE), jnp.bfloat16), pltpu.VMEM((512, 128), jnp.float32),
-         pltpu.VMEM((2, 256, 256), jnp.float32)],
-        600_000,
-        2200,
-    )
-
-
-def fore_sums(x, weights, before, wb, first, tiles):
+        in_specs=[pl.BlockSpec(memory_space=pltpu.HBM)] * 7,
+        out_specs=[NEAR] * 9,
+        out_shape=[
+            f32(272, 128), near(512, points), wide(16, points), wide(512, points),
+            wide(512, points), near(784, 256), near(points, 256), near(points, 256),
+            near(points, 256),
+        ],
+        scratch_shapes=[
+            pltpu.VMEM((512, FIRST_TILE), jnp.bfloat16), pltpu.VMEM((512, 128), jnp.float32),
+            pltpu.VMEM((2, 256, 256), jnp.float32), pltpu.VMEM((256, 512), jnp.bfloat16),
+            pltpu.VMEM((256, 256), jnp.bfloat16), pltpu.VMEM((8, 256), jnp.bfloat16),
+            pltpu.VMEM((256, 256), jnp.bfloat16),
+            pltpu.SemaphoreType.DMA((5 + 2 * (points // FIRST_TILE),)),
+        ],
+        compiler_params=pltpu.CompilerParams(vmem_limit_bytes=VMEM_LIMIT),
+        cost_estimate=pl.CostEstimate(
+            flops=1_200_000 * points, bytes_accessed=2200 * points, transcendentals=0
+        ),
+    )(*operands)
+
+
+def fore_sums(x, weights):
     points = x.shape[0]
-    earlier = [] if wb is None else [(wb, pl.BlockSpec(memory_space=pl.ANY))]
-    return call(
+    return pl.pallas_call(
         fore_sums_kernel,
-        tiles * TILE,
-        TILE,
-        [(x, rows_of(TILE, 256, first)), (weights, NEAR), (before, NEAR)] + earlier,
-        [(f32(144, 128), NEAR), (pltpu.HBM((512, points), jnp.bfloat16), columns_of(TILE, 512, first))],
-        [pltpu.VMEM((512, 128), jnp.float32), pltpu.VMEM((2, 256, 128), jnp.float32),
-         pltpu.VMEM((256, TILE), jnp.bfloat16)],
-        500_000,
-        1500,
-        {} if wb is None else {3: 1},
-    )
-
-
-def back_grads(sums, mix, x, cot, weights, vo, stats):
+        in_specs=[NEAR, NEAR],
+        out_specs=[NEAR, NEAR],
+        out_shape=[f32(144, 128), near(512, points)],
+        scratch_shapes=[
+            pltpu.VMEM((512, 128), jnp.float32), pltpu.VMEM((2, 256, 128), jnp.float32),
+            pltpu.VMEM((256, TILE), jnp.bfloat16),
+        ],
+        compiler_params=pltpu.CompilerParams(vmem_limit_bytes=VMEM_LIMIT),
+        cost_estimate=pl.CostEstimate(
+            flops=1_000_000 * points, bytes_accessed=1500 * points, transcendentals=0
+        ),
+    )(x, weights)
+
+
+def back_grads(sums, mix, x, cot, vo, stats, w, below, fore_wb):
     points = x.shape[0]
     tile = GRAD_TILE
     return call(
         back_grads_kernel,
         points,
         tile,
-        [(sums, NEAR), (mix, NEAR), (x, rows_of(tile, 256)), (cot, rows_of(tile, 256)),
-         (weights, NEAR), (vo, NEAR), (stats, NEAR)],
-        [(f32(256, 1152), NEAR), (f32(512, 128), NEAR), (pltpu.HBM((784, points), jnp.bfloat16), columns_of(tile, 784))],
+        [(sums, NEAR), (mix, NEAR), (x, NEAR), (cot, NEAR),
+         (vo, NEAR), (stats, NEAR), (w, NEAR), (below, NEAR),
+         (fore_wb, NEAR)],
+        [(near(16, 8, 1152, dtype=jnp.float32), NEAR), (near(16, 8, 1152, dtype=jnp.float32), NEAR),
+         (pltpu.HBM((784, points), jnp.bfloat16), columns_of(tile, 784)),
+         (pltpu.HBM((512, points), jnp.bfloat16), pl.BlockSpec(memory_space=pltpu.HBM))],
         [pltpu.VMEM((2, 256, 256), jnp.bfloat16), pltpu.VMEM((2, 256, 256), jnp.bfloat16),
          pltpu.VMEM((512, 128), jnp.float32), pltpu.VMEM((512, tile), jnp.bfloat16),
          pltpu.VMEM((256, tile), jnp.bfloat16), pltpu.VMEM((8, tile), jnp.float32),
-         pltpu.VMEM((784, 256), jnp.float32), pltpu.VMEM((256, 256), jnp.float32)],
+         pltpu.VMEM((784, 256), jnp.float32), pltpu.VMEM((256, 256), jnp.float32),
+         pltpu.VMEM((256, 1152), jnp.float32), pltpu.SemaphoreType.DMA],
         800_000,
         3800,
     )
@@ -522,6 +547,16 @@
     return small_call(mix_maps_kernel, [f32(512, 128), f32(256, 128)], w_mix.T)
 
 
+def gram_kernel(sums_ref, gram_ref):
+    lane = lax.broadcasted_iota(jnp.int32, (M, 128), 1)
+    first = lane % 64 < HEAD_SIZE
+    inverse = inverse_denominators(sums_ref[256:264, 0:M])
+    for q in range(4):
+        scale = jnp.where(lane < 64, inverse[2 * q], inverse[2 * q + 1])
+        scaled = sums_ref[q * M : (q + 1) * M, :] * jnp.where(first, scale, 1.0)
+        gram_ref[q * 128 : (q + 1) * 128, :] = dot_exact(scaled, scaled, ((0,), (0,)))
+
+
 def own_mixing_rows(gram):
     point = lax.axis_index("point")
     odd = point // 4 % 2
@@ -532,7 +567,7 @@
 
 def join_kernel(parts_ref, own_ref, out_ref):
     total = parts_ref[0]
-    for k in range(1, 32):
+    for k in range(1, 16):
         total = total + parts_ref[k]
     for k in range(8):
         out_ref[k, :, :] = total
@@ -563,36 +598,42 @@
     fore_x = fore_points[0]
     back_x = back_points[0]
     cot = cotangent[0]
-    turned_temp = w_temp.T
-
-    sums, vo, stats, weights = back_sums(back_x, cot, w_slice, w_value, turned_temp, w_out)
+    even = lax.axis_index("point") % 2 == 0
+    turned_temp, even = tie(w_temp.T, even)
+
+    sums, vo, stats, w, below, weights, near_x, near_cot, near_fore = back_sums(
+        back_x, cot, w_slice, w_value, turned_temp, w_out, fore_x
+    )
     sums, turned_mix = tie(sums, w_mix)
-    half = row_halves(sums)
+    half = row_halves(sums, even)
     back_map, fore_map = mix_maps(turned_mix)
-    half, back_map, fore = tie(half, back_map, jnp.zeros((144, 128), jnp.float32))
+    half, back_map, weights = tie(half, back_map, weights)
     half = quad_sum(half, along_x)
-    fore, fore_wb = fore_sums(fore_x, weights, fore, None, 0, 1)
+    fore, fore_wb = fore_sums(near_fore, weights)
     half, fore = tie(half, fore)
     half = quad_sum(half, along_y)
-    fore, fore_wb = fore_sums(fore_x, weights, fore, fore_wb, 1, 1)
+    fore = pair_sum(pair_sum(fore, CORE_SWAP), along_x(1))
     half, fore = tie(half, fore)
-    sums = both_halves(half)
-    fore_half = row_halves(fore)
-    sums, fore_half = tie(sums, fore_half)
-    fore_half = pair_sum(fore_half, along_x(1))
-
-    wide, gram, stack = back_grads(sums, back_map, back_x, cot, weights, vo, stats)
-    wide, gram, fore_half, turned_temp = tie(wide, gram, fore_half, turned_temp)
-    parts = lax.all_to_all(wide.reshape(32, 8, 1152), "point", 0, 0)
-    own_mix = own_mixing_rows(gram)
-    fore_half = pair_sum(fore_half, along_x(3))
+    sums = both_halves(half, even)
+    received = lax.ppermute(fore, "point", along_x(3))
+
+    keep, send, stack, fore_wb = back_grads(
+        sums, back_map, near_x, near_cot, vo, stats, w, below, fore_wb
+    )
+    send, sums, received, turned_temp = tie(send, sums, received, turned_temp)
+    fore = fore + received
+    blocks = keep + lax.ppermute(send, "point", CORE_SWAP)
+    chips = [[i for i in range(32) if i % 2 == core] for core in range(2)]
+    parts = lax.all_to_all(blocks, "point", 0, 0, axis_index_groups=chips)
+    own_mix = own_mixing_rows(small_call(gram_kernel, f32(512, 128), sums))
+    fore = pair_sum(fore, along_y(1))
     grad_points = grad_of_points(stack, w_slice, w_value, turned_temp)
-    fore_half, grad_points, own_mix = tie(fore_half, grad_points, own_mix)
-    fore_half = pair_sum(fore_half, along_y(1))
-    parts, fore_half = tie(parts, fore_half)
-    parts = lax.all_to_all(join(parts, own_mix), "dp", 0, 0)
-    fore = both_halves(pair_sum(fore_half, along_y(3)))
-    fore_result = fore_results(fore, fore_map, fore_wb, w_out)
+    fore, grad_points, own_mix, parts = tie(fore, grad_points, own_mix, parts)
+    received = lax.ppermute(fore, "point", along_y(3))
+    joined = join(parts, own_mix)
+    parts = lax.all_to_all(joined, "dp", 0, 0)
+    joined, received = tie(joined, received)
+    fore_result = fore_results(fore + received, fore_map, fore_wb, w_out)
     parts, fore_result = tie(parts, fore_result)
     value_rows, slice_rows, temp_rows, mix_rows, out_rows = finish(parts)
     return (

time: 95.8 us -> 83.7 us (0.87); the launches traced: 94.3 us -> 83.4 us
  Pallas kernels: 42.6 us -> 35.7 us
  starting transfers between devices: 34.3 us -> 31.8 us
  waiting for transfers between devices: 16.3 us -> 13.9 us
    pallas_call x6 -> x3, Pallas kernels: 40.6 us -> 21.3 us  [call(): pl.pallas_call(kernel, grid=(points // tile,), in_specs=[spec for _, spec...]
    ppermute x4 -> x3, waiting for transfers between devices: 13.5 us -> 1.59 us  [pair_sum(): return half + lax.ppermute(half, 'point', pairs)]
    pallas_call x0 -> x2, Pallas kernels: none -> 11.8 us  [the longest x1 6.82 us: back_sums(): pl.pallas_call(back_sums_kernel, in_specs=[pl.BlockSpec(memory_space=pltp...]
    ppermute x2 -> x4, waiting for transfers between devices: 1.46 us -> 7.55 us  [the longest x1 4.99 us: local(): received = lax.ppermute(fore, 'point', along_y(3))]
    ppermute x4 -> x3, starting transfers between devices: 9.6 us -> 4.34 us  [pair_sum(): return half + lax.ppermute(half, 'point', pairs)]
    ppermute x2 -> x4, starting transfers between devices: 0.19 us -> 3.14 us  [the longest x1 2.18 us: local(): received = lax.ppermute(fore, 'point', along_x(3))]
    all_to_all x2, waiting for transfers between devices: 0.01 us -> 2.42 us  [the longest x1 2.41 us: local(): parts = lax.all_to_all(blocks, 'point', 0, 0, axis_index_groups=chips)]
    ppermute x6, waiting for transfers between devices: 0.02 us -> 2.34 us  [quad_sum(): parts = [lax.ppermute(half, 'point', pairs(flip)) for flip in (1, 3, 2)]]
  transfers between devices with their start and end apart: 16 -> 16, of which waited for: 7 -> 6; matrix products, arithmetic and copies ran while one was open for 0% -> 0% of each run, Pallas kernels for 36% -> 33%
where the time goes in v2:
time: 83.7 us; the launch traced here: 83.4 us
  Pallas kernels  35.7 us (43%)
  starting transfers between devices  31.8 us (38%)
  waiting for transfers between devices  13.9 us (17%)
  other arithmetic  1.02 us (1%)
  between operations  0.88 us (1%)
    pallas_call x3, Pallas kernels, call(): pl.pallas_call(kernel, grid=(points // tile,), in_specs=[spec for _, spec...  21.3 us
    ppermute x6, starting transfers between devices, quad_sum(): parts = [lax.ppermute(half, 'point', pairs(flip)) for flip in (1, 3, 2)]  8.59 us
    all_to_all x1, starting transfers between devices, local(): parts = lax.all_to_all(joined, 'dp', 0, 0)  8.59 us
    all_to_all x1, starting transfers between devices, local(): parts = lax.all_to_all(blocks, 'point', 0, 0, axis_index_groups=chips)  7.02 us
    pallas_call x1, Pallas kernels, back_sums(): pl.pallas_call(back_sums_kernel, in_specs=[pl.BlockSpec(memory_space=pltp...  6.82 us
    pallas_call x1, Pallas kernels, fore_sums(): pl.pallas_call(fore_sums_kernel, in_specs=[NEAR, NEAR], out_specs=[NEAR,...  4.99 us
    ppermute x1, waiting for transfers between devices, local(): received = lax.ppermute(fore, 'point', along_y(3))  4.99 us
    ppermute x3, starting transfers between devices, pair_sum(): return half + lax.ppermute(half, 'point', pairs)  4.34 us
  transfers between devices with their start and end apart: 16, of which 6 were waited for; matrix products, arithmetic and copies ran while one was open for 0% of the time, Pallas kernels for 33%

profile of v2, /device:TPU:32, one launch (start us, length us, event | category | flops | bytes accessed | tf_op | source)
XLA Modules:
  0.0 83.4 jit_solution(15076452559325698877)
XLA Ops:
  0.7 6.8 %shard_map.135 = (f32[272,128]{1,0:T(8,128)S(1)}, bf16[512,4096]{1,0:T(8,128)(2,1)S(1)}, f32[16,4096]{1,0:T(8,128)S(1)}, f32[512,4096]{1,0:T(8,128)S(1)}, f32[51...) custom-call(bf16[4096,256]{1,0:T(8,128)(2,1)} %bitcast.12, ...), custom_call_target="tpu_custom_call" | custom-call | flops 4915200000 | bytes 9011200 | tf_op jit(solution)/shard_map/pallas_call | solution.py:417
  8.1 0.8 collective-permute-done
  8.9 3.1 %collective-permute-start.3 = (f32[136,128]{1,0:T(8,128)S(1)}, f32[136,128]{1,0:T(8,128)S(1)}, u32[]{:S(2)}, u32[]{:S(2)}) collective-permute-start(f32[136,128]{1,0:T(8,128)S(1)} %select_add_fusion), channel_id=1, source_target_pairs={{0,16},{1,17},{2,18},{3,19},{4,20},{5,21},{6,22},{7,23},{8,24},{9,... | collective-permute-start | bytes 208904 | tf_op jit(solution)/shard_map/ppermute | solution.py:48
  12.0 1.1 %collective-permute-start.2 = (f32[136,128]{1,0:T(8,128)S(1)}, f32[136,128]{1,0:T(8,128)S(1)}, u32[]{:S(2)}, u32[]{:S(2)}) collective-permute-start(f32[136,128]{1,0:T(8,128)S(1)} %select_add_fusion), channel_id=1, source_target_pairs={{0,24},{1,25},{2,26},{3,27},{4,28},{5,29},{6,30},{7,31},{8,16},{9,... | collective-permute-start | bytes 208904 | tf_op jit(solution)/shard_map/ppermute | solution.py:48
  13.1 5.0 %shard_map.137 = (f32[144,128]{1,0:T(8,128)S(1)}, bf16[512,4096]{1,0:T(8,128)(2,1)S(1)}) custom-call(bf16[4096,256]{1,0:T(8,128)(2,1)S(1)} %get-tuple-element.59.x_ref, bf16[784,256]{1,0:T(8,128)(2,1)S(1)} %get-tuple-element.60.weights_ref), custom_call_target="tpu_custom_call" | custom-call | flops 4096000000 | bytes 6144000 | tf_op jit(solution)/shard_map/pallas_call | solution.py:442
  18.5 3.3 %collective-permute-start.6 = (f32[136,128]{1,0:T(8,128)S(1)}, f32[136,128]{1,0:T(8,128)S(1)}, u32[]{:S(2)}, u32[]{:S(2)}) collective-permute-start(f32[136,128]{1,0:T(8,128)S(1)} %add_add_fusion.1), channel_id=1, source_target_pairs={{0,4},{1,5},{2,6},{3,7},{4,0},{5,1},{6,2},{7,3},{8,12},{9,13},{10,... | collective-permute-start | bytes 208904 | tf_op jit(solution)/shard_map/ppermute | solution.py:48
  21.7 1.1 %collective-permute-start.5 = (f32[136,128]{1,0:T(8,128)S(1)}, f32[136,128]{1,0:T(8,128)S(1)}, u32[]{:S(2)}, u32[]{:S(2)}) collective-permute-start(f32[136,128]{1,0:T(8,128)S(1)} %add_add_fusion.1), channel_id=1, source_target_pairs={{0,6},{1,7},{2,4},{3,5},{4,2},{5,3},{6,0},{7,1},{8,14},{9,15},{10,... | collective-permute-start | bytes 208904 | tf_op jit(solution)/shard_map/ppermute | solution.py:48
  22.8 2.1 %collective-permute-start.8 = (f32[144,128]{1,0:T(8,128)S(1)}, f32[144,128]{1,0:T(8,128)S(1)}, u32[]{:S(2)}, u32[]{:S(2)}) collective-permute-start(f32[144,128]{1,0:T(8,128)S(1)} %add.78), channel_id=1, source_target_pairs={{0,8},{1,9},{2,10},{3,11},{4,12},{5,13},{6,14},{7,15},{8,0},{9,1},... | collective-permute-start | bytes 221192 | tf_op jit(solution)/shard_map/ppermute | solution.py:44
  24.9 2.3 %collective-permute-done.5 = f32[136,128]{1,0:T(8,128)S(1)} collective-permute-done((f32[136,128]{1,0:T(8,128)S(1)}, f32[136,128]{1,0:T(8,128)S(1)}, u32[]{:S(2)}, u32[]{:S(2)}) %collective-permute-start.5) | collective-permute-done | bytes 69664 | tf_op jit(solution)/shard_map/ppermute | solution.py:48
  27.4 2.2 %collective-permute-start.10 = (f32[144,128]{1,0:T(8,128)S(1)}, f32[144,128]{1,0:T(8,128)S(1)}, u32[]{:S(2)}, u32[]{:S(2)}) collective-permute-start(f32[144,128]{1,0:T(8,128)S(1)} %add.79), channel_id=1, source_target_pairs={{0,24},{1,25},{2,26},{3,27},{4,28},{5,29},{6,30},{7,31},{8,16},{9,... | collective-permute-start | bytes 221192 | tf_op jit(solution)/shard_map/ppermute | solution.py:618
  29.6 10.8 %shard_map.138 = (f32[16,8,1152]{2,1,0:T(8,128)S(1)}, f32[16,8,1152]{2,1,0:T(8,128)S(1)}, bf16[784,4096]{1,0:T(8,128)(2,1)}, bf16[512,4096]{1,0:T(8,128)(2,1)}) custom-call(f32[272,128]{1,0:T(8,128)S(1)} %pad_maximum_fusion.sums_ref, f32[512,128]{1,0:T(8,128)S(1)} %get-tuple-element.66.mix_ref, bf16[4096,256]{1,0:T(8,128)(2,1)S(1)} %get-tuple-element.67.x_ref, ...), custom_call_target="tpu_custom_call" | custom-call | flops 6553600000 | bytes 15564800 | tf_op jit(solution)/shard_map/pallas_call | solution.py:395
  40.7 1.8 %collective-permute-done.12 = f32[16,8,1152]{2,1,0:T(8,128)S(1)} collective-permute-done((f32[16,8,1152]{2,1,0:T(8,128)S(1)}, f32[16,8,1152]{2,1,0:T(8,128)S(1)}, u32[]{:S(2)}, u32[]{:S(2)}) %collective-permute-start.12) | collective-permute-done | bytes 589856 | tf_op jit(solution)/shard_map/ppermute | solution.py:625
  42.5 0.9 %add.89 = f32[16,8,1152]{2,1,0:T(8,128)} add(f32[16,8,1152]{2,1,0:T(8,128)S(1)} %get-tuple-element.79, f32[16,8,1152]{2,1,0:T(8,128)S(1)} %collective-permute-done.12) | non-fusion elementwise | flops 147456 | bytes 1769472 | tf_op jit(solution)/shard_map/add | solution.py:625
  43.4 7.0 %all-to-all-start = ((f32[16,8,1152]{2,1,0:T(8,128)}), f32[16,8,1152]{2,1,0:T(8,128)S(1)}, u32[]{:S(2)}, u32[]{:S(2)}) async-start(f32[16,8,1152]{2,1,0:T(8,128)} %add.89), calls=%async_computation | async-start | bytes 1179648 | tf_op jit(solution)/shard_map/all_to_all | solution.py:627
  50.5 2.0 %collective-permute-start.11 = (f32[144,128]{1,0:T(8,128)S(1)}, f32[144,128]{1,0:T(8,128)S(1)}, u32[]{:S(2)}, u32[]{:S(2)}) collective-permute-start(f32[144,128]{1,0:T(8,128)S(1)} %add.80), channel_id=1, source_target_pairs={{0,2},{1,3},{2,0},{3,1},{4,6},{5,7},{6,4},{7,5},{8,10},{9,11},{10,... | collective-permute-start | bytes 221192 | tf_op jit(solution)/shard_map/ppermute | solution.py:44
  52.5 5.7 %shard_map.139 = bf16[4096,256]{1,0:T(8,128)(2,1)} custom-call(bf16[784,4096]{1,0:T(8,128)(2,1)} %get-tuple-element.76.stack_ref, bf16[256,512]{1,0:T(8,128)(2,1)} %ws_ref.1, bf16[256,256]{1,0:T(8,128)(2,1)} %wv_ref.1, bf16[8,256]{1,0:T(8,128)(2,1)} %bitcast.11), custom_call_target="tpu_custom_call" | custom-call | flops 1638400000 | bytes 8601600 | tf_op jit(solution)/shard_map/pallas_call | solution.py:395
  58.2 0.7 shard_map.140
  59.0 1.6 %collective-permute-done.11 = f32[144,128]{1,0:T(8,128)S(1)} collective-permute-done((f32[144,128]{1,0:T(8,128)S(1)}, f32[144,128]{1,0:T(8,128)S(1)}, u32[]{:S(2)}, u32[]{:S(2)}) %collective-permute-start.11) | collective-permute-done | bytes 73760 | tf_op jit(solution)/shard_map/ppermute | solution.py:44
  60.6 2.4 %all-to-all-done.parts_ref = f32[16,8,1152]{2,1,0:T(8,128)S(1)} async-done(((f32[16,8,1152]{2,1,0:T(8,128)}), f32[16,8,1152]{2,1,0:T(8,128)S(1)}, u32[]{:S(2)}, u32[]{:S(2)}) %all-to-all-start) | async-done | bytes 589856 | tf_op jit(solution)/shard_map/all_to_all | solution.py:627
  63.0 0.8 shard_map.141
  63.8 8.6 %all-to-all-start.1 = ((f32[8,8,1152]{2,1,0:T(8,128)}), f32[8,8,1152]{2,1,0:T(8,128)S(1)}, u32[]{:S(2)}, u32[]{:S(2)}) async-start(f32[8,8,1152]{2,1,0:T(8,128)} %shard_map.141), calls=%async_computation.1 | async-start | bytes 589824 | tf_op jit(solution)/shard_map/all_to_all | solution.py:634
  72.9 5.0 %collective-permute-done.13 = f32[144,128]{1,0:T(8,128)S(1)} collective-permute-done((f32[144,128]{1,0:T(8,128)S(1)}, f32[144,128]{1,0:T(8,128)S(1)}, u32[]{:S(2)}, u32[]{:S(2)}) %collective-permute-start.13) | collective-permute-done | bytes 73760 | tf_op jit(solution)/shard_map/ppermute | solution.py:632
  77.9 4.8 %shard_map.142 = bf16[4096,256]{1,0:T(8,128)(2,1)} custom-call(f32[144,128]{1,0:T(8,128)S(1)} %add.90.sums_ref, f32[256,128]{1,0:T(8,128)S(1)} %get-tuple-element.85.mix_ref, bf16[512,4096]{1,0:T(8,128)(2,1)} %get-tuple-element.86.wb_ref, bf16[256,256]{1,0:T(8,128)(2,1)} %wo_ref.1), custom_call_target="tpu_custom_call" | custom-call | flops 1064960000 | bytes 6553600 | tf_op jit(solution)/shard_map/pallas_call | solution.py:395
  82.7 0.7 shard_map.143
  (33 shorter events, 2.1 us)
Async XLA Ops:
  0.6 7.0 %copy-start = (f32[256,32]{0,1:T(8,128)S(1)}, f32[256,32]{0,1:T(8,128)}, u32[]{:S(2)}) copy-start(f32[256,32]{0,1:T(8,128)} %param.14) | copy-start | bytes 98308
  7.5 1.3 %collective-permute-start = (f32[136,128]{1,0:T(8,128)S(1)}, f32[136,128]{1,0:T(8,128)S(1)}, u32[]{:S(2)}, u32[]{:S(2)}) collective-permute-start(f32[136,128]{1,0:T(8,128)S(1)} %slice_select_fusion), channel_id=1, source_target_pairs={{0,1},{1,0},{2,3},{3,2},{4,5},{5,4},{6,7},{7,6},{8,9},{9,8},{10,11... | collective-permute-start | bytes 208904 | tf_op jit(solution)/shard_map/ppermute | solution.py:40
  8.9 9.3 %collective-permute-start.3 = (f32[136,128]{1,0:T(8,128)S(1)}, f32[136,128]{1,0:T(8,128)S(1)}, u32[]{:S(2)}, u32[]{:S(2)}) collective-permute-start(f32[136,128]{1,0:T(8,128)S(1)} %select_add_fusion), channel_id=1, source_target_pairs={{0,16},{1,17},{2,18},{3,19},{4,20},{5,21},{6,22},{7,23},{8,24},{9,... | collective-permute-start | bytes 208904 | tf_op jit(solution)/shard_map/ppermute | solution.py:48
  12.0 6.1 %collective-permute-start.2 = (f32[136,128]{1,0:T(8,128)S(1)}, f32[136,128]{1,0:T(8,128)S(1)}, u32[]{:S(2)}, u32[]{:S(2)}) collective-permute-start(f32[136,128]{1,0:T(8,128)S(1)} %select_add_fusion), channel_id=1, source_target_pairs={{0,24},{1,25},{2,26},{3,27},{4,28},{5,29},{6,30},{7,31},{8,16},{9,... | collective-permute-start | bytes 208904 | tf_op jit(solution)/shard_map/ppermute | solution.py:48
  13.1 5.0 %collective-permute-start.1 = (f32[136,128]{1,0:T(8,128)S(1)}, f32[136,128]{1,0:T(8,128)S(1)}, u32[]{:S(2)}, u32[]{:S(2)}) collective-permute-start(f32[136,128]{1,0:T(8,128)S(1)} %select_add_fusion), channel_id=1, source_target_pairs={{0,8},{1,9},{2,10},{3,11},{4,12},{5,13},{6,14},{7,15},{8,0},{9,1},... | collective-permute-start | bytes 208904 | tf_op jit(solution)/shard_map/ppermute | solution.py:48
  18.2 4.6 %collective-permute-start.7 = (f32[144,128]{1,0:T(8,128)S(1)}, f32[144,128]{1,0:T(8,128)S(1)}, u32[]{:S(2)}, u32[]{:S(2)}) collective-permute-start(f32[144,128]{1,0:T(8,128)S(1)} %get-tuple-element.63), channel_id=1, source_target_pairs={{0,1},{1,0},{2,3},{3,2},{4,5},{5,4},{6,7},{7,6},{8,9},{9,8},{10,11... | collective-permute-start | bytes 221192 | tf_op jit(solution)/shard_map/ppermute | solution.py:44
  18.5 6.5 %collective-permute-start.6 = (f32[136,128]{1,0:T(8,128)S(1)}, f32[136,128]{1,0:T(8,128)S(1)}, u32[]{:S(2)}, u32[]{:S(2)}) collective-permute-start(f32[136,128]{1,0:T(8,128)S(1)} %add_add_fusion.1), channel_id=1, source_target_pairs={{0,4},{1,5},{2,6},{3,7},{4,0},{5,1},{6,2},{7,3},{8,12},{9,13},{10,... | collective-permute-start | bytes 208904 | tf_op jit(solution)/shard_map/ppermute | solution.py:48
  21.7 5.5 %collective-permute-start.5 = (f32[136,128]{1,0:T(8,128)S(1)}, f32[136,128]{1,0:T(8,128)S(1)}, u32[]{:S(2)}, u32[]{:S(2)}) collective-permute-start(f32[136,128]{1,0:T(8,128)S(1)} %add_add_fusion.1), channel_id=1, source_target_pairs={{0,6},{1,7},{2,4},{3,5},{4,2},{5,3},{6,0},{7,1},{8,14},{9,15},{10,... | collective-permute-start | bytes 208904 | tf_op jit(solution)/shard_map/ppermute | solution.py:48
  22.8 4.5 %collective-permute-start.4 = (f32[136,128]{1,0:T(8,128)S(1)}, f32[136,128]{1,0:T(8,128)S(1)}, u32[]{:S(2)}, u32[]{:S(2)}) collective-permute-start(f32[136,128]{1,0:T(8,128)S(1)} %add_add_fusion.1), channel_id=1, source_target_pairs={{0,2},{1,3},{2,0},{3,1},{4,6},{5,7},{6,4},{7,5},{8,10},{9,11},{10,... | collective-permute-start | bytes 208904 | tf_op jit(solution)/shard_map/ppermute | solution.py:48
  22.8 4.5 %collective-permute-start.8 = (f32[144,128]{1,0:T(8,128)S(1)}, f32[144,128]{1,0:T(8,128)S(1)}, u32[]{:S(2)}, u32[]{:S(2)}) collective-permute-start(f32[144,128]{1,0:T(8,128)S(1)} %add.78), channel_id=1, source_target_pairs={{0,8},{1,9},{2,10},{3,11},{4,12},{5,13},{6,14},{7,15},{8,0},{9,1},... | collective-permute-start | bytes 221192 | tf_op jit(solution)/shard_map/ppermute | solution.py:44
  27.3 2.3 %collective-permute-start.9 = (f32[136,128]{1,0:T(8,128)S(1)}, f32[136,128]{1,0:T(8,128)S(1)}, u32[]{:S(2)}, u32[]{:S(2)}) collective-permute-start(f32[136,128]{1,0:T(8,128)S(1)} %add_add_fusion), channel_id=1, source_target_pairs={{0,1},{1,0},{2,3},{3,2},{4,5},{5,4},{6,7},{7,6},{8,9},{9,8},{10,11... | collective-permute-start | bytes 208904 | tf_op jit(solution)/shard_map/ppermute | solution.py:53
  27.4 13.0 %collective-permute-start.10 = (f32[144,128]{1,0:T(8,128)S(1)}, f32[144,128]{1,0:T(8,128)S(1)}, u32[]{:S(2)}, u32[]{:S(2)}) collective-permute-start(f32[144,128]{1,0:T(8,128)S(1)} %add.79), channel_id=1, source_target_pairs={{0,24},{1,25},{2,26},{3,27},{4,28},{5,29},{6,30},{7,31},{8,16},{9,... | collective-permute-start | bytes 221192 | tf_op jit(solution)/shard_map/ppermute | solution.py:618
  40.4 2.1 %collective-permute-start.12 = (f32[16,8,1152]{2,1,0:T(8,128)S(1)}, f32[16,8,1152]{2,1,0:T(8,128)S(1)}, u32[]{:S(2)}, u32[]{:S(2)}) collective-permute-start(f32[16,8,1152]{2,1,0:T(8,128)S(1)} %get-tuple-element.80), channel_id=1, source_target_pairs={{0,1},{1,0},{2,3},{3,2},{4,5},{5,4},{6,7},{7,6},{8,9},{9,8},{10,11... | collective-permute-start | bytes 1769480 | tf_op jit(solution)/shard_map/ppermute | solution.py:625
  43.4 19.6 %all-to-all-start = ((f32[16,8,1152]{2,1,0:T(8,128)}), f32[16,8,1152]{2,1,0:T(8,128)S(1)}, u32[]{:S(2)}, u32[]{:S(2)}) async-start(f32[16,8,1152]{2,1,0:T(8,128)} %add.89), calls=%async_computation | async-start | bytes 1179648 | tf_op jit(solution)/shard_map/all_to_all | solution.py:627
  50.5 10.1 %collective-permute-start.11 = (f32[144,128]{1,0:T(8,128)S(1)}, f32[144,128]{1,0:T(8,128)S(1)}, u32[]{:S(2)}, u32[]{:S(2)}) collective-permute-start(f32[144,128]{1,0:T(8,128)S(1)} %add.80), channel_id=1, source_target_pairs={{0,2},{1,3},{2,0},{3,1},{4,6},{5,7},{6,4},{7,5},{8,10},{9,11},{10,... | collective-permute-start | bytes 221192 | tf_op jit(solution)/shard_map/ppermute | solution.py:44
  63.8 19.0 %all-to-all-start.1 = ((f32[8,8,1152]{2,1,0:T(8,128)}), f32[8,8,1152]{2,1,0:T(8,128)S(1)}, u32[]{:S(2)}, u32[]{:S(2)}) async-start(f32[8,8,1152]{2,1,0:T(8,128)} %shard_map.141), calls=%async_computation.1 | async-start | bytes 589824 | tf_op jit(solution)/shard_map/all_to_all | solution.py:634
  72.3 5.6 %collective-permute-start.13 = (f32[144,128]{1,0:T(8,128)S(1)}, f32[144,128]{1,0:T(8,128)S(1)}, u32[]{:S(2)}, u32[]{:S(2)}) collective-permute-start(f32[144,128]{1,0:T(8,128)S(1)} %add.81), channel_id=1, source_target_pairs={{0,6},{1,7},{2,4},{3,5},{4,2},{5,3},{6,0},{7,1},{8,14},{9,15},{10,... | collective-permute-start | bytes 221192 | tf_op jit(solution)/shard_map/ppermute | solution.py:632

commit v3 on v2

--- a/solution.py
+++ b/solution.py
@@ -337,27 +337,42 @@
     out_ref[...] = dot_nn(wide[...], stack_ref[...]).T.astype(jnp.bfloat16)
 
 
-def fore_result_kernel(sums_ref, mix_ref, wb_ref, wo_ref, out_ref, blocks_t, wo_t):
-    @pl.when(pl.program_id(0) == 0)
-    def _():
-        wo_t[...] = wo_ref[...].T
-        lane = lax.broadcasted_iota(jnp.int32, (M, 128), 1)
-        inverse = inverse_denominators(sums_ref[128:136, 0:M])
-        for g in range(2):
-            scale = jnp.zeros((M, 128), jnp.float32)
-            for j in range(4):
-                scale = jnp.where(lane // HEAD_SIZE == j, inverse[g * 4 + j], scale)
-            tokens = sums_ref[g * M : (g + 1) * M, :] * scale
-            mixed = dot_exact(tokens, mix_ref[g * 128 : (g + 1) * 128, :], ((1,), (0,)))
-            rows = [jnp.where(lane // HEAD_SIZE == j, mixed, 0.0) for j in range(4)]
-            blocks_t[g, :, :] = jnp.concatenate(rows, axis=0).T.astype(jnp.bfloat16)
-
-    parts = [
-        dot_nn(blocks_t[g, :, :], wb_ref[g * 256 : (g + 1) * 256, :]).astype(jnp.bfloat16)
-        for g in range(2)
-    ]
-    out = dot_nn(wo_t[...], jnp.concatenate(parts, axis=0))
-    out_ref[...] = out.T.astype(jnp.bfloat16)
+def fore_result_kernel(
+    sums_ref, mix_ref, wb_far, wo_far, out_far, blocks_t, wo_t, wo, wb, out, sems
+):
+    def fetch(source, target, k):
+        copy = pltpu.make_async_copy(source, target, sems.at[k])
+        copy.start()
+        return copy
+
+    bounds = [0, TILE // 2, out.shape[0] - TILE // 2, out.shape[0]]
+    tiles = [pl.ds(a, b - a) for a, b in zip(bounds, bounds[1:])]
+    wo_copy = fetch(wo_far, wo, 0)
+    arriving = [fetch(wb_far.at[:, t], wb.at[:, t], 1 + k) for k, t in enumerate(tiles)]
+    lane = lax.broadcasted_iota(jnp.int32, (M, 128), 1)
+    inverse = inverse_denominators(sums_ref[128:136, 0:M])
+    for g in range(2):
+        scale = jnp.zeros((M, 128), jnp.float32)
+        for j in range(4):
+            scale = jnp.where(lane // HEAD_SIZE == j, inverse[g * 4 + j], scale)
+        tokens = sums_ref[g * M : (g + 1) * M, :] * scale
+        mixed = dot_exact(tokens, mix_ref[g * 128 : (g + 1) * 128, :], ((1,), (0,)))
+        rows = [jnp.where(lane // HEAD_SIZE == j, mixed, 0.0) for j in range(4)]
+        blocks_t[g, :, :] = jnp.concatenate(rows, axis=0).T.astype(jnp.bfloat16)
+    wo_copy.wait()
+    wo_t[...] = wo[...].T
+    leaving = []
+    for k, t in enumerate(tiles):
+        arriving[k].wait()
+        parts = [
+            dot_nn(blocks_t[g, :, :], wb[g * 256 : (g + 1) * 256, t]).astype(jnp.bfloat16)
+            for g in range(2)
+        ]
+        product = dot_nn(wo_t[...], jnp.concatenate(parts, axis=0))
+        out[t, :] = product.T.astype(jnp.bfloat16)
+        leaving.append(fetch(out.at[t], out_far.at[t], 4 + k))
+    for copy in leaving:
+        copy.wait()
 
 
 def f32(*shape):
@@ -495,16 +510,22 @@
 
 def fore_results(sums, mix, wb, w_out):
     points = wb.shape[1]
-    return call(
+    far = pl.BlockSpec(memory_space=pltpu.HBM)
+    return pl.pallas_call(
         fore_result_kernel,
-        points,
-        TILE,
-        [(sums, NEAR), (mix, NEAR), (wb, columns_of(TILE, 512)), (w_out, whole(256, 256))],
-        [(bf16(points, 256), rows_of(TILE, 256))],
-        [pltpu.VMEM((2, 128, 256), jnp.bfloat16), pltpu.VMEM((256, 256), jnp.bfloat16)],
-        130_000,
-        1600,
-    )[0]
+        in_specs=[NEAR, NEAR, far, far],
+        out_specs=far,
+        out_shape=pltpu.HBM((points, 256), jnp.bfloat16),
+        scratch_shapes=[
+            pltpu.VMEM((2, 128, 256), jnp.bfloat16), pltpu.VMEM((256, 256), jnp.bfloat16),
+            pltpu.VMEM((256, 256), jnp.bfloat16), pltpu.VMEM((512, points), jnp.bfloat16),
+            pltpu.VMEM((points, 256), jnp.bfloat16), pltpu.SemaphoreType.DMA((7,)),
+        ],
+        compiler_params=pltpu.CompilerParams(vmem_limit_bytes=VMEM_LIMIT),
+        cost_estimate=pl.CostEstimate(
+            flops=260_000 * points, bytes_accessed=1600 * points, transcendentals=0
+        ),
+    )(sums, mix, *(pltpu.with_memory_space_constraint(a, pltpu.HBM) for a in (wb, w_out)))
 
 
 def one_hot(rows, columns, hit):

time: 83.7 us -> 83.5 us (level)
    pallas_call x3 -> x2, Pallas kernels: 21.3 us -> 16.5 us  [call(): pl.pallas_call(kernel, grid=(points // tile,), in_specs=[spec for _, spec...]
    pallas_call x0 -> x1, Pallas kernels: none -> 4.54 us  [fore_results(): pl.pallas_call(fore_result_kernel, in_specs=[NEAR, NEAR, far, far], out_s...]
where the time goes in v3:
time: 83.5 us; the launch traced here: 83.2 us
  Pallas kernels  35.4 us (42%)
  starting transfers between devices  31.8 us (38%)
  waiting for transfers between devices  13.9 us (17%)
  other arithmetic  1.02 us (1%)
  between operations  0.9 us (1%)
    pallas_call x2, Pallas kernels, call(): pl.pallas_call(kernel, grid=(points // tile,), in_specs=[spec for _, spec...  16.5 us
    ppermute x6, starting transfers between devices, quad_sum(): parts = [lax.ppermute(half, 'point', pairs(flip)) for flip in (1, 3, 2)]  8.59 us
    all_to_all x1, starting transfers between devices, local(): parts = lax.all_to_all(joined, 'dp', 0, 0)  8.59 us
    all_to_all x1, starting transfers between devices, local(): parts = lax.all_to_all(blocks, 'point', 0, 0, axis_index_groups=chips)  7.02 us
    pallas_call x1, Pallas kernels, back_sums(): pl.pallas_call(back_sums_kernel, in_specs=[pl.BlockSpec(memory_space=pltp...  6.82 us
    pallas_call x1, Pallas kernels, fore_sums(): pl.pallas_call(fore_sums_kernel, in_specs=[NEAR, NEAR], out_specs=[NEAR,...  4.99 us
    ppermute x1, waiting for transfers between devices, local(): received = lax.ppermute(fore, 'point', along_y(3))  4.99 us
    pallas_call x1, Pallas kernels, fore_results(): pl.pallas_call(fore_result_kernel, in_specs=[NEAR, NEAR, far, far], out_s...  4.54 us
  transfers between devices with their start and end apart: 16, of which 6 were waited for; matrix products, arithmetic and copies ran while one was open for 0% of the time, Pallas kernels for 33%

profile of v3, /device:TPU:32, one launch (start us, length us, event | category | flops | bytes accessed | tf_op | source)
XLA Modules:
  0.0 83.2 jit_solution(1453548338154935424)
XLA Ops:
  0.7 6.8 %shard_map.135 = (f32[272,128]{1,0:T(8,128)S(1)}, bf16[512,4096]{1,0:T(8,128)(2,1)S(1)}, f32[16,4096]{1,0:T(8,128)S(1)}, f32[512,4096]{1,0:T(8,128)S(1)}, f32[51...) custom-call(bf16[4096,256]{1,0:T(8,128)(2,1)} %bitcast.12, ...), custom_call_target="tpu_custom_call" | custom-call | flops 4915200000 | bytes 9011200 | tf_op jit(solution)/shard_map/pallas_call | solution.py:432
  8.1 0.8 collective-permute-done
  8.9 3.1 %collective-permute-start.3 = (f32[136,128]{1,0:T(8,128)S(1)}, f32[136,128]{1,0:T(8,128)S(1)}, u32[]{:S(2)}, u32[]{:S(2)}) collective-permute-start(f32[136,128]{1,0:T(8,128)S(1)} %select_add_fusion), channel_id=1, source_target_pairs={{0,16},{1,17},{2,18},{3,19},{4,20},{5,21},{6,22},{7,23},{8,24},{9,... | collective-permute-start | bytes 208904 | tf_op jit(solution)/shard_map/ppermute | solution.py:48
  12.0 1.1 %collective-permute-start.2 = (f32[136,128]{1,0:T(8,128)S(1)}, f32[136,128]{1,0:T(8,128)S(1)}, u32[]{:S(2)}, u32[]{:S(2)}) collective-permute-start(f32[136,128]{1,0:T(8,128)S(1)} %select_add_fusion), channel_id=1, source_target_pairs={{0,24},{1,25},{2,26},{3,27},{4,28},{5,29},{6,30},{7,31},{8,16},{9,... | collective-permute-start | bytes 208904 | tf_op jit(solution)/shard_map/ppermute | solution.py:48
  13.1 5.0 %shard_map.137 = (f32[144,128]{1,0:T(8,128)S(1)}, bf16[512,4096]{1,0:T(8,128)(2,1)S(1)}) custom-call(bf16[4096,256]{1,0:T(8,128)(2,1)S(1)} %get-tuple-element.59.x_ref, bf16[784,256]{1,0:T(8,128)(2,1)S(1)} %get-tuple-element.60.weights_ref), custom_call_target="tpu_custom_call" | custom-call | flops 4096000000 | bytes 6144000 | tf_op jit(solution)/shard_map/pallas_call | solution.py:457
  18.5 3.3 %collective-permute-start.6 = (f32[136,128]{1,0:T(8,128)S(1)}, f32[136,128]{1,0:T(8,128)S(1)}, u32[]{:S(2)}, u32[]{:S(2)}) collective-permute-start(f32[136,128]{1,0:T(8,128)S(1)} %add_add_fusion.1), channel_id=1, source_target_pairs={{0,4},{1,5},{2,6},{3,7},{4,0},{5,1},{6,2},{7,3},{8,12},{9,13},{10,... | collective-permute-start | bytes 208904 | tf_op jit(solution)/shard_map/ppermute | solution.py:48
  21.7 1.1 %collective-permute-start.5 = (f32[136,128]{1,0:T(8,128)S(1)}, f32[136,128]{1,0:T(8,128)S(1)}, u32[]{:S(2)}, u32[]{:S(2)}) collective-permute-start(f32[136,128]{1,0:T(8,128)S(1)} %add_add_fusion.1), channel_id=1, source_target_pairs={{0,6},{1,7},{2,4},{3,5},{4,2},{5,3},{6,0},{7,1},{8,14},{9,15},{10,... | collective-permute-start | bytes 208904 | tf_op jit(solution)/shard_map/ppermute | solution.py:48
  22.8 2.1 %collective-permute-start.8 = (f32[144,128]{1,0:T(8,128)S(1)}, f32[144,128]{1,0:T(8,128)S(1)}, u32[]{:S(2)}, u32[]{:S(2)}) collective-permute-start(f32[144,128]{1,0:T(8,128)S(1)} %add.78), channel_id=1, source_target_pairs={{0,8},{1,9},{2,10},{3,11},{4,12},{5,13},{6,14},{7,15},{8,0},{9,1},... | collective-permute-start | bytes 221192 | tf_op jit(solution)/shard_map/ppermute | solution.py:44
  24.9 2.3 %collective-permute-done.5 = f32[136,128]{1,0:T(8,128)S(1)} collective-permute-done((f32[136,128]{1,0:T(8,128)S(1)}, f32[136,128]{1,0:T(8,128)S(1)}, u32[]{:S(2)}, u32[]{:S(2)}) %collective-permute-start.5) | collective-permute-done | bytes 69664 | tf_op jit(solution)/shard_map/ppermute | solution.py:48
  27.4 2.2 %collective-permute-start.10 = (f32[144,128]{1,0:T(8,128)S(1)}, f32[144,128]{1,0:T(8,128)S(1)}, u32[]{:S(2)}, u32[]{:S(2)}) collective-permute-start(f32[144,128]{1,0:T(8,128)S(1)} %add.79), channel_id=1, source_target_pairs={{0,24},{1,25},{2,26},{3,27},{4,28},{5,29},{6,30},{7,31},{8,16},{9,... | collective-permute-start | bytes 221192 | tf_op jit(solution)/shard_map/ppermute | solution.py:639
  29.6 10.8 %shard_map.138 = (f32[16,8,1152]{2,1,0:T(8,128)S(1)}, f32[16,8,1152]{2,1,0:T(8,128)S(1)}, bf16[784,4096]{1,0:T(8,128)(2,1)}, bf16[512,4096]{1,0:T(8,128)(2,1)}) custom-call(f32[272,128]{1,0:T(8,128)S(1)} %pad_maximum_fusion.sums_ref, f32[512,128]{1,0:T(8,128)S(1)} %get-tuple-element.66.mix_ref, bf16[4096,256]{1,0:T(8,128)(2,1)S(1)} %get-tuple-element.67.x_ref, ...), custom_call_target="tpu_custom_call" | custom-call | flops 6553600000 | bytes 15564800 | tf_op jit(solution)/shard_map/pallas_call | solution.py:410
  40.7 1.8 %collective-permute-done.12 = f32[16,8,1152]{2,1,0:T(8,128)S(1)} collective-permute-done((f32[16,8,1152]{2,1,0:T(8,128)S(1)}, f32[16,8,1152]{2,1,0:T(8,128)S(1)}, u32[]{:S(2)}, u32[]{:S(2)}) %collective-permute-start.12) | collective-permute-done | bytes 589856 | tf_op jit(solution)/shard_map/ppermute | solution.py:646
  42.5 0.9 %add.89 = f32[16,8,1152]{2,1,0:T(8,128)} add(f32[16,8,1152]{2,1,0:T(8,128)S(1)} %get-tuple-element.79, f32[16,8,1152]{2,1,0:T(8,128)S(1)} %collective-permute-done.12) | non-fusion elementwise | flops 147456 | bytes 1769472 | tf_op jit(solution)/shard_map/add | solution.py:646
  43.4 7.0 %all-to-all-start = ((f32[16,8,1152]{2,1,0:T(8,128)}), f32[16,8,1152]{2,1,0:T(8,128)S(1)}, u32[]{:S(2)}, u32[]{:S(2)}) async-start(f32[16,8,1152]{2,1,0:T(8,128)} %add.89), calls=%async_computation | async-start | bytes 1179648 | tf_op jit(solution)/shard_map/all_to_all | solution.py:648
  50.5 2.0 %collective-permute-start.11 = (f32[144,128]{1,0:T(8,128)S(1)}, f32[144,128]{1,0:T(8,128)S(1)}, u32[]{:S(2)}, u32[]{:S(2)}) collective-permute-start(f32[144,128]{1,0:T(8,128)S(1)} %add.80), channel_id=1, source_target_pairs={{0,2},{1,3},{2,0},{3,1},{4,6},{5,7},{6,4},{7,5},{8,10},{9,11},{10,... | collective-permute-start | bytes 221192 | tf_op jit(solution)/shard_map/ppermute | solution.py:44
  52.5 5.7 %shard_map.139 = bf16[4096,256]{1,0:T(8,128)(2,1)} custom-call(bf16[784,4096]{1,0:T(8,128)(2,1)} %get-tuple-element.76.stack_ref, bf16[256,512]{1,0:T(8,128)(2,1)} %ws_ref.1, bf16[256,256]{1,0:T(8,128)(2,1)} %wv_ref.1, bf16[8,256]{1,0:T(8,128)(2,1)} %bitcast.11), custom_call_target="tpu_custom_call" | custom-call | flops 1638400000 | bytes 8601600 | tf_op jit(solution)/shard_map/pallas_call | solution.py:410
  58.2 0.7 shard_map.140
  59.0 1.6 %collective-permute-done.11 = f32[144,128]{1,0:T(8,128)S(1)} collective-permute-done((f32[144,128]{1,0:T(8,128)S(1)}, f32[144,128]{1,0:T(8,128)S(1)}, u32[]{:S(2)}, u32[]{:S(2)}) %collective-permute-start.11) | collective-permute-done | bytes 73760 | tf_op jit(solution)/shard_map/ppermute | solution.py:44
  60.6 2.4 %all-to-all-done.parts_ref = f32[16,8,1152]{2,1,0:T(8,128)S(1)} async-done(((f32[16,8,1152]{2,1,0:T(8,128)}), f32[16,8,1152]{2,1,0:T(8,128)S(1)}, u32[]{:S(2)}, u32[]{:S(2)}) %all-to-all-start) | async-done | bytes 589856 | tf_op jit(solution)/shard_map/all_to_all | solution.py:648
  63.0 0.8 shard_map.141
  63.8 8.6 %all-to-all-start.1 = ((f32[8,8,1152]{2,1,0:T(8,128)}), f32[8,8,1152]{2,1,0:T(8,128)S(1)}, u32[]{:S(2)}, u32[]{:S(2)}) async-start(f32[8,8,1152]{2,1,0:T(8,128)} %shard_map.141), calls=%async_computation.1 | async-start | bytes 589824 | tf_op jit(solution)/shard_map/all_to_all | solution.py:655
  72.9 5.0 %collective-permute-done.13 = f32[144,128]{1,0:T(8,128)S(1)} collective-permute-done((f32[144,128]{1,0:T(8,128)S(1)}, f32[144,128]{1,0:T(8,128)S(1)}, u32[]{:S(2)}, u32[]{:S(2)}) %collective-permute-start.13) | collective-permute-done | bytes 73760 | tf_op jit(solution)/shard_map/ppermute | solution.py:653
  77.9 4.5 %shard_map.142 = bf16[4096,256]{1,0:T(8,128)(2,1)} custom-call(f32[144,128]{1,0:T(8,128)S(1)} %add.90.sums_ref, f32[256,128]{1,0:T(8,128)S(1)} %get-tuple-element.85.mix_ref, bf16[512,4096]{1,0:T(8,128)(2,1)} %get-tuple-element.86.wb_far, bf16[256,256]{1,0:T(8,128)(2,1)} %wo_far.3), custom_call_target="tpu_custom_call" | custom-call | flops 1064960000 | bytes 6553600 | tf_op jit(solution)/shard_map/pallas_call | solution.py:514
  82.5 0.7 shard_map.143
  (33 shorter events, 2.1 us)
Async XLA Ops:
  0.6 7.0 %copy-start = (f32[256,32]{0,1:T(8,128)S(1)}, f32[256,32]{0,1:T(8,128)}, u32[]{:S(2)}) copy-start(f32[256,32]{0,1:T(8,128)} %param.14) | copy-start | bytes 98308
  7.5 1.3 %collective-permute-start = (f32[136,128]{1,0:T(8,128)S(1)}, f32[136,128]{1,0:T(8,128)S(1)}, u32[]{:S(2)}, u32[]{:S(2)}) collective-permute-start(f32[136,128]{1,0:T(8,128)S(1)} %slice_select_fusion), channel_id=1, source_target_pairs={{0,1},{1,0},{2,3},{3,2},{4,5},{5,4},{6,7},{7,6},{8,9},{9,8},{10,11... | collective-permute-start | bytes 208904 | tf_op jit(solution)/shard_map/ppermute | solution.py:40
  8.9 9.3 %collective-permute-start.3 = (f32[136,128]{1,0:T(8,128)S(1)}, f32[136,128]{1,0:T(8,128)S(1)}, u32[]{:S(2)}, u32[]{:S(2)}) collective-permute-start(f32[136,128]{1,0:T(8,128)S(1)} %select_add_fusion), channel_id=1, source_target_pairs={{0,16},{1,17},{2,18},{3,19},{4,20},{5,21},{6,22},{7,23},{8,24},{9,... | collective-permute-start | bytes 208904 | tf_op jit(solution)/shard_map/ppermute | solution.py:48
  12.0 6.1 %collective-permute-start.2 = (f32[136,128]{1,0:T(8,128)S(1)}, f32[136,128]{1,0:T(8,128)S(1)}, u32[]{:S(2)}, u32[]{:S(2)}) collective-permute-start(f32[136,128]{1,0:T(8,128)S(1)} %select_add_fusion), channel_id=1, source_target_pairs={{0,24},{1,25},{2,26},{3,27},{4,28},{5,29},{6,30},{7,31},{8,16},{9,... | collective-permute-start | bytes 208904 | tf_op jit(solution)/shard_map/ppermute | solution.py:48
  13.1 5.0 %collective-permute-start.1 = (f32[136,128]{1,0:T(8,128)S(1)}, f32[136,128]{1,0:T(8,128)S(1)}, u32[]{:S(2)}, u32[]{:S(2)}) collective-permute-start(f32[136,128]{1,0:T(8,128)S(1)} %select_add_fusion), channel_id=1, source_target_pairs={{0,8},{1,9},{2,10},{3,11},{4,12},{5,13},{6,14},{7,15},{8,0},{9,1},... | collective-permute-start | bytes 208904 | tf_op jit(solution)/shard_map/ppermute | solution.py:48
  18.2 4.6 %collective-permute-start.7 = (f32[144,128]{1,0:T(8,128)S(1)}, f32[144,128]{1,0:T(8,128)S(1)}, u32[]{:S(2)}, u32[]{:S(2)}) collective-permute-start(f32[144,128]{1,0:T(8,128)S(1)} %get-tuple-element.63), channel_id=1, source_target_pairs={{0,1},{1,0},{2,3},{3,2},{4,5},{5,4},{6,7},{7,6},{8,9},{9,8},{10,11... | collective-permute-start | bytes 221192 | tf_op jit(solution)/shard_map/ppermute | solution.py:44
  18.5 6.5 %collective-permute-start.6 = (f32[136,128]{1,0:T(8,128)S(1)}, f32[136,128]{1,0:T(8,128)S(1)}, u32[]{:S(2)}, u32[]{:S(2)}) collective-permute-start(f32[136,128]{1,0:T(8,128)S(1)} %add_add_fusion.1), channel_id=1, source_target_pairs={{0,4},{1,5},{2,6},{3,7},{4,0},{5,1},{6,2},{7,3},{8,12},{9,13},{10,... | collective-permute-start | bytes 208904 | tf_op jit(solution)/shard_map/ppermute | solution.py:48
  21.7 5.5 %collective-permute-start.5 = (f32[136,128]{1,0:T(8,128)S(1)}, f32[136,128]{1,0:T(8,128)S(1)}, u32[]{:S(2)}, u32[]{:S(2)}) collective-permute-start(f32[136,128]{1,0:T(8,128)S(1)} %add_add_fusion.1), channel_id=1, source_target_pairs={{0,6},{1,7},{2,4},{3,5},{4,2},{5,3},{6,0},{7,1},{8,14},{9,15},{10,... | collective-permute-start | bytes 208904 | tf_op jit(solution)/shard_map/ppermute | solution.py:48
  22.8 4.5 %collective-permute-start.4 = (f32[136,128]{1,0:T(8,128)S(1)}, f32[136,128]{1,0:T(8,128)S(1)}, u32[]{:S(2)}, u32[]{:S(2)}) collective-permute-start(f32[136,128]{1,0:T(8,128)S(1)} %add_add_fusion.1), channel_id=1, source_target_pairs={{0,2},{1,3},{2,0},{3,1},{4,6},{5,7},{6,4},{7,5},{8,10},{9,11},{10,... | collective-permute-start | bytes 208904 | tf_op jit(solution)/shard_map/ppermute | solution.py:48
  22.8 4.5 %collective-permute-start.8 = (f32[144,128]{1,0:T(8,128)S(1)}, f32[144,128]{1,0:T(8,128)S(1)}, u32[]{:S(2)}, u32[]{:S(2)}) collective-permute-start(f32[144,128]{1,0:T(8,128)S(1)} %add.78), channel_id=1, source_target_pairs={{0,8},{1,9},{2,10},{3,11},{4,12},{5,13},{6,14},{7,15},{8,0},{9,1},... | collective-permute-start | bytes 221192 | tf_op jit(solution)/shard_map/ppermute | solution.py:44
  27.3 2.3 %collective-permute-start.9 = (f32[136,128]{1,0:T(8,128)S(1)}, f32[136,128]{1,0:T(8,128)S(1)}, u32[]{:S(2)}, u32[]{:S(2)}) collective-permute-start(f32[136,128]{1,0:T(8,128)S(1)} %add_add_fusion), channel_id=1, source_target_pairs={{0,1},{1,0},{2,3},{3,2},{4,5},{5,4},{6,7},{7,6},{8,9},{9,8},{10,11... | collective-permute-start | bytes 208904 | tf_op jit(solution)/shard_map/ppermute | solution.py:53
  27.4 13.0 %collective-permute-start.10 = (f32[144,128]{1,0:T(8,128)S(1)}, f32[144,128]{1,0:T(8,128)S(1)}, u32[]{:S(2)}, u32[]{:S(2)}) collective-permute-start(f32[144,128]{1,0:T(8,128)S(1)} %add.79), channel_id=1, source_target_pairs={{0,24},{1,25},{2,26},{3,27},{4,28},{5,29},{6,30},{7,31},{8,16},{9,... | collective-permute-start | bytes 221192 | tf_op jit(solution)/shard_map/ppermute | solution.py:639
  40.4 2.1 %collective-permute-start.12 = (f32[16,8,1152]{2,1,0:T(8,128)S(1)}, f32[16,8,1152]{2,1,0:T(8,128)S(1)}, u32[]{:S(2)}, u32[]{:S(2)}) collective-permute-start(f32[16,8,1152]{2,1,0:T(8,128)S(1)} %get-tuple-element.80), channel_id=1, source_target_pairs={{0,1},{1,0},{2,3},{3,2},{4,5},{5,4},{6,7},{7,6},{8,9},{9,8},{10,11... | collective-permute-start | bytes 1769480 | tf_op jit(solution)/shard_map/ppermute | solution.py:646
  43.4 19.6 %all-to-all-start = ((f32[16,8,1152]{2,1,0:T(8,128)}), f32[16,8,1152]{2,1,0:T(8,128)S(1)}, u32[]{:S(2)}, u32[]{:S(2)}) async-start(f32[16,8,1152]{2,1,0:T(8,128)} %add.89), calls=%async_computation | async-start | bytes 1179648 | tf_op jit(solution)/shard_map/all_to_all | solution.py:648
  50.5 10.1 %collective-permute-start.11 = (f32[144,128]{1,0:T(8,128)S(1)}, f32[144,128]{1,0:T(8,128)S(1)}, u32[]{:S(2)}, u32[]{:S(2)}) collective-permute-start(f32[144,128]{1,0:T(8,128)S(1)} %add.80), channel_id=1, source_target_pairs={{0,2},{1,3},{2,0},{3,1},{4,6},{5,7},{6,4},{7,5},{8,10},{9,11},{10,... | collective-permute-start | bytes 221192 | tf_op jit(solution)/shard_map/ppermute | solution.py:44
  63.8 18.7 %all-to-all-start.1 = ((f32[8,8,1152]{2,1,0:T(8,128)}), f32[8,8,1152]{2,1,0:T(8,128)S(1)}, u32[]{:S(2)}, u32[]{:S(2)}) async-start(f32[8,8,1152]{2,1,0:T(8,128)} %shard_map.141), calls=%async_computation.1 | async-start | bytes 589824 | tf_op jit(solution)/shard_map/all_to_all | solution.py:655
  72.3 5.6 %collective-permute-start.13 = (f32[144,128]{1,0:T(8,128)S(1)}, f32[144,128]{1,0:T(8,128)S(1)}, u32[]{:S(2)}, u32[]{:S(2)}) collective-permute-start(f32[144,128]{1,0:T(8,128)S(1)} %add.81), channel_id=1, source_target_pairs={{0,6},{1,7},{2,4},{3,5},{4,2},{5,3},{6,0},{7,1},{8,14},{9,15},{10,... | collective-permute-start | bytes 221192 | tf_op jit(solution)/shard_map/ppermute | solution.py:653
